TPU v7x, 32 devices: a whole 2x2x4 slice. The times are simulated.
32 devices in a mesh: req: 8 (over z, x), tp: 4 (over y, core).
Axes of the slice: x: 2, y: 2, z: 4, core: 2. Of those that a mesh axis runs over, the one named last changes fastest.
Arguments:
- tokens_new: bfloat16 [8, 16, 2, 1024], P('req'), may hold values from -6 to 6
- prefix_len: int32 [8], replicated, may hold values from 1 to 4096, as said below
- tail_len: int32 [8, 16], P('req'), may hold values from 1 to 512, as said below
- pool_home: int32 [256], replicated, may hold values from 0 to 7, as said below
- pool_page: int32 [256], replicated, may hold values from 0 to 31
- slot_page_cache: bfloat16 [256, 128, 2, 512], P('req', None, None, 'tp'), may hold values from -64 to 64
- tail_cache: bfloat16 [8, 16, 512, 2, 512], P('req', None, None, None, 'tp'), may hold values from -6 to 6
- routes: int32 [8, 16, 2, 8], P('req'), may hold values from 0 to 31, all different within a row; in each aligned block of 32 rows (0 to 31, 32 to 63, ..., all dimensions but the last counted through in order) at most 12 rows name the same one
- norm_gains: float32 [3, 1024], replicated, may hold values from 0.1 to 1.9
- query_weight: bfloat16 [1024, 1024], P(None, 'tp'), may hold values from -0.1875 to 0.1875
- key_value_weight: bfloat16 [1024, 2, 512], P(None, None, 'tp'), may hold values from -0.1875 to 0.1875
- out_weight: bfloat16 [1024, 1024], P('tp'), may hold values from -0.1875 to 0.1875
- router: bfloat16 [1024, 32], replicated, may hold values from -0.375 to 0.375
- expert_in: bfloat16 [32, 1024, 2, 512], P('req', None, None, 'tp'), as said below
- expert_out: bfloat16 [32, 512, 1024], P('req', 'tp'), as said below
- score_weight: float32 [1024], replicated, may hold values from -0.1875 to 0.1875
Outputs:
- layer_out: bfloat16 [8, 16, 2, 1024], P('req')
- row_score: float32 [8, 16, 2], P('req')
Inputs may be any that keep to these rules, and one draw needn't show every extreme that they name: `prefix_len`: some request has exactly 4096 prefix positions. `tail_len`: some sample has exactly 512 tail positions. `pool_home`: entry s * 32 + v describes slot v of the pool of device s of req. Every page 0 to 31 of every request lies in exactly one slot, and one device's pool holds either exactly 4 pages of a request or none of them. `routes`: in the 32 rows of one device no expert is named more than 12 times. `expert_in`: expert table copy c equals copy c mod 32. `expert_out`: expert table copy c equals copy c mod 32.
All inputs are finite; a program needn't handle non-finite values.
Results may differ from a plain program's by a relative error of at most 0.017.
Values may be sent and summed in bfloat16 or wider, within the bound.
No kernel may reach another device: no remote copies, remote signals or barrier semaphores. Data moves between devices by JAX's collectives and lax.ppermute only.
A program may use at most 128 MiB of HBM per device.

v0:
```python
import functools
import math

import jax
import jax.numpy as jnp
from jax import lax
from jax.experimental import pallas as pl
from jax.experimental.pallas import tpu as pltpu
from jax.sharding import PartitionSpec as P

HEAD_DIM = 64
LANES = 128
EPSILON = 1e-05
ROPE_BASE = 10000.0
LOWEST = -1e30
FLOOR = -1e28
F32 = jnp.float32
BF16 = jnp.bfloat16
MIB = 1024 * 1024
HOLD_MIB = 56

VMEM = pl.BlockSpec(memory_space=pltpu.VMEM)
SMEM = pl.BlockSpec(memory_space=pltpu.SMEM)
HBM = pl.BlockSpec(memory_space=pltpu.HBM)
ANY = pl.BlockSpec(memory_space=pl.ANY)


def params(mib):
    return pltpu.CompilerParams(vmem_limit_bytes=mib * MIB)


def cost(flops, moved):
    return pl.CostEstimate(flops=int(flops), bytes_accessed=int(moved), transcendentals=0)


def dot(left, right):
    return jnp.dot(left, right, preferred_element_type=F32)


def dot_t(left, right):
    return lax.dot_general(left, right, (((1,), (1,)), ((), ())), preferred_element_type=F32)


def my_part():
    return lax.axis_index("tp_pair") * 2 + lax.axis_index("tp_side")


def load_all(pairs, done):
    copies = [pltpu.make_async_copy(far, near, done.at[k]) for k, (far, near) in enumerate(pairs)]
    for copy in copies:
        copy.start()
    return copies


def lane_iota(shape):
    return lax.broadcasted_iota(jnp.int32, shape, len(shape) - 1)


def normalize(x, gain):
    return x * lax.rsqrt(jnp.mean(x * x, axis=-1, keepdims=True) + EPSILON) * gain


def rotate(x, cosine, sine):
    lanes = lane_iota(x.shape)
    partner = jnp.where(lanes % HEAD_DIM < HEAD_DIM // 2, pltpu.roll(x, 96, 1), pltpu.roll(x, 32, 1))
    return x * cosine + partner * sine


def by_head(packed, low):
    zero = jnp.zeros_like(packed)
    return jnp.concatenate([jnp.where(low, packed, zero), jnp.where(low, zero, packed)], axis=0)


def swap_halves(first, second):
    low = lane_iota(first.shape) < HEAD_DIM
    return (
        jnp.where(low, first, pltpu.roll(second, HEAD_DIM, 1)),
        jnp.where(low, pltpu.roll(first, HEAD_DIM, 1), second),
    )


def query_kernel(
    fresh_count,
    prefix_far,
    lengths_far,
    tokens_far,
    named_far,
    gains_far,
    weight_far,
    message,
    flat,
    normed,
    cosine,
    sine,
    prefix,
    lengths,
    tokens,
    named,
    gains,
    weight,
    wide,
    ordered,
    done,
):
    loads = load_all(
        (
            (tokens_far, tokens),
            (gains_far, gains),
            (lengths_far, lengths),
            (prefix_far, prefix),
            (weight_far, weight),
            (named_far, named),
        ),
        done,
    )
    count, model = normed.shape
    samples = count // fresh_count
    parts, part_rows, _ = flat.shape
    blocks = model // LANES
    loads[0].wait()
    wide[...] = tokens[...].astype(F32)
    for c in range(blocks):
        for i in range(fresh_count):
            ordered[c, pl.ds(i, samples, stride=fresh_count), :] = wide[
                pl.ds(fresh_count * c + i, samples, stride=fresh_count * blocks), :
            ]
    states = jnp.concatenate([ordered[c] for c in range(blocks)], axis=1)
    for part in range(parts):
        flat[part] = states[part * part_rows : (part + 1) * part_rows].astype(BF16)
    loads[1].wait()
    rows = normalize(states, gains[0:1, :]).astype(BF16)
    normed[...] = rows
    loads[2].wait()
    loads[3].wait()
    row_id = lax.broadcasted_iota(jnp.int32, (count, 1), 0)
    position = row_id % fresh_count + prefix[lax.axis_index("req")]
    for sample in range(samples):
        position = position + jnp.where(row_id // fresh_count == sample, lengths[0, sample], 0)
    within = lane_iota((1, LANES)) % HEAD_DIM
    pair = (within % (HEAD_DIM // 2)).astype(F32)
    frequency = jnp.exp(pair * (-math.log(ROPE_BASE) / (HEAD_DIM // 2)))
    angles = position.astype(F32) * frequency
    cosine[...] = jnp.cos(angles)
    turn = jnp.sin(angles)
    sine[...] = jnp.where(within < HEAD_DIM // 2, -turn, turn)
    loads[4].wait()
    made = dot(rows, weight[...])
    pieces = []
    for group in swap_halves(made[:, :LANES], made[:, LANES:]):
        pieces.append(rotate(group, cosine[...], sine[...]).astype(BF16).astype(F32) * 0.125)
    packed = []
    for part in range(parts):
        for piece in pieces:
            packed.append(piece[part * part_rows : (part + 1) * part_rows])
    loads[5].wait()
    routed = named[...].astype(F32)
    packed.append(
        jnp.concatenate(
            [routed, jnp.zeros((routed.shape[0], LANES - routed.shape[1]), F32)], axis=1
        )
    )
    packed = jnp.concatenate(packed, axis=0).astype(BF16)
    for n in range(message.shape[0]):
        message[n] = packed


def split_pages_kernel(source, out, wide):
    count, double, _ = source.shape
    half = double // 2
    wide[...] = source[...].astype(F32).reshape(count * double, LANES)
    keys = wide[pl.ds(0, count * half, stride=2), :].astype(BF16)
    values = wide[pl.ds(1, count * half, stride=2), :].astype(BF16)
    out[:, :half, :] = keys.reshape(count, half, LANES)
    out[:, half:, :] = values.reshape(count, half, LANES)


def pack_message(numer, top, total):
    high = total.astype(BF16).astype(F32)
    section = (lane_iota((8, LANES)) % HEAD_DIM) // 8
    stats = jnp.zeros((8, LANES), F32)
    for group in range(2):
        span = slice(group * 8, (group + 1) * 8)
        for k, kind in enumerate((top, high, total - high)):
            stats = jnp.where(section == 3 * group + k, kind[span], stats)
    return jnp.concatenate([numer, stats], axis=0).astype(BF16)


def unpack_message(block):
    block = block.astype(F32)
    stats = block[..., 16:24, :]
    low = lane_iota(stats.shape) < HEAD_DIM

    def pick(section):
        lane = section * 8
        return jnp.where(
            low, stats[..., lane : lane + 1], stats[..., HEAD_DIM + lane : HEAD_DIM + lane + 1]
        )

    top = jnp.concatenate([pick(0), pick(3)], axis=-2)
    total = jnp.concatenate([pick(1) + pick(2), pick(4) + pick(5)], axis=-2)
    return block[..., 0:16, :], top, total


def tail_kernel(
    fresh_count,
    lengths_far,
    query_far,
    normed_far,
    cosine_far,
    sine_far,
    weight_far,
    cache_far,
    out,
    lengths,
    query,
    normed,
    cosine,
    sine,
    weight,
    cache,
    load,
    done,
):
    tokens = normed.shape[0]
    samples, width, _ = cache.shape
    parts = out.shape[0]
    per_part = samples // parts
    loads = load_all(
        (
            (normed_far, normed),
            (weight_far, weight),
            (cosine_far, cosine),
            (sine_far, sine),
            (query_far.at[0, pl.ds(0, parts * 16)], query),
            (lengths_far, lengths),
        ),
        load,
    )
    spans = [pl.ds(part * per_part, per_part) for part in range(parts)]
    blocks = load_all([(cache_far.at[span], cache.at[span]) for span in spans], done)
    spread = (
        lax.broadcasted_iota(jnp.int32, (LANES, 2 * LANES), 1)
        == 2 * lax.broadcasted_iota(jnp.int32, (LANES, 2 * LANES), 0)
    ).astype(BF16)
    loads[0].wait()
    rows = normed[...]
    widened = jnp.concatenate(
        [dot(rows[:, c : c + LANES], spread) for c in range(0, rows.shape[1], LANES)], axis=1
    )
    both = jnp.concatenate([widened, pltpu.roll(widened, 1, 1)], axis=0).astype(BF16)
    for copy in loads[1:]:
        copy.wait()
    made = dot(both, weight[...])
    key_new = rotate(made[:tokens], cosine[...], sine[...]).astype(BF16)
    value_new = made[tokens:].astype(BF16)
    low = lane_iota((16, LANES)) < HEAD_DIM
    row_id = lax.broadcasted_iota(jnp.int32, (parts * 32, 1), 0)
    row_sample = (row_id // 32) * per_part + (row_id % 8) // fresh_count
    row_fresh = row_id % fresh_count
    part_sample = row_sample[:32]
    wide = [by_head(query[part * 16 : (part + 1) * 16, :], low) for part in range(parts)]
    length = jnp.zeros((parts * 32, 1), jnp.int32)
    for sample in range(samples):
        length = jnp.where(row_sample == sample, lengths[0, sample], length)
    fresh = dot_t(jnp.concatenate(wide, axis=0), key_new)
    token_id = lane_iota(fresh.shape)
    fresh_seen = (token_id // fresh_count == row_sample) & (token_id % fresh_count <= row_fresh)
    fresh = jnp.where(fresh_seen, fresh, LOWEST)
    for copy in blocks:
        copy.wait()
    beside = []
    scores = []
    for part in range(parts):
        placed = [
            jnp.where(part_sample == a, wide[part], jnp.zeros_like(wide[part]))
            for a in range(per_part)
        ]
        beside.append(
            jnp.concatenate([cache[part * per_part + a] for a in range(per_part)], axis=1)
        )
        scores.append(dot_t(jnp.concatenate(placed, axis=1), beside[part]))
    scores = jnp.concatenate(scores, axis=0)
    column = lane_iota(scores.shape)
    scores = jnp.where((column % 2 == 0) & (column < 2 * length), scores, LOWEST)
    peak = jnp.maximum(
        jnp.max(scores, axis=1, keepdims=True), jnp.max(fresh, axis=1, keepdims=True)
    )
    peak = peak.astype(BF16).astype(F32)
    weights = jnp.exp(scores - peak)
    fresh_weights = jnp.exp(fresh - peak)
    amount = jnp.sum(weights, axis=1, keepdims=True) + jnp.sum(fresh_weights, axis=1, keepdims=True)
    shifted = pltpu.roll(weights, 1, 1).astype(BF16)
    fresh_part = dot(fresh_weights.astype(BF16), value_new)
    every = [dot(shifted[part * 32 : (part + 1) * 32], beside[part]) for part in range(parts)]
    for part in range(parts):
        mixed = every[part][:, :LANES]
        for a in range(1, per_part):
            mixed = jnp.where(part_sample == a, every[part][:, a * LANES : (a + 1) * LANES], mixed)
        first = slice(part * 32, part * 32 + 16)
        second = slice(part * 32 + 16, part * 32 + 32)
        mixed = mixed + fresh_part[part * 32 : (part + 1) * 32]
        out[part] = pack_message(
            jnp.where(low, mixed[:16], mixed[16:]),
            jnp.where(low, peak[first], peak[second]),
            jnp.where(low, amount[first], amount[second]),
        )


def page_kernel(
    slot_cap, homes, pages, lengths, cache, tail, query, out, named, slots, counts
):
    requests = query.shape[0]
    parts = tail.shape[0]
    pool = cache.shape[0]
    page_size = cache.shape[1] // 2
    rows = parts * 16
    me = lax.axis_index("req")
    base = me * pool
    tail_numer, tail_top, tail_total = [
        kind.reshape(rows, LANES) for kind in unpack_message(tail[...])
    ]
    named[...] = query[:, rows:, :]

    def clear(r, carry):
        counts[r] = 0
        for j in range(slot_cap):
            slots[r * slot_cap + j] = -1
        return carry

    lax.fori_loop(0, requests, clear, 0)

    def assign(v, carry):
        r = homes[base + v]
        rank = counts[r]
        slots[r * slot_cap + rank] = v
        counts[r] = rank + 1
        return carry

    lax.fori_loop(0, pool, assign, 0)

    low = lane_iota((rows, LANES)) < HEAD_DIM
    column = lane_iota((2 * rows, page_size))

    def finish(r, mixed, peak, amount):
        own = r == me
        top = jnp.where(low, peak[:rows], peak[rows:])
        joint = jnp.maximum(top, jnp.where(own, tail_top, FLOOR))
        here = jnp.exp(top - joint)
        there = jnp.where(own, jnp.exp(tail_top - joint), 0.0)
        numer = jnp.where(low, mixed[:rows], mixed[rows:]) * here + tail_numer * there
        total = jnp.where(low, amount[:rows], amount[rows:]) * here + tail_total * there
        for part in range(parts):
            span = slice(part * 16, (part + 1) * 16)
            out[r * parts + part] = pack_message(numer[span], joint[span], total[span])

    def gather(first, count):
        wides = []
        keys = []
        values = []
        limits = []
        for k in range(count):
            r = first + k
            wide = by_head(query[r, 0:rows, :], low)
            zero = jnp.zeros_like(wide)
            wides.append(jnp.concatenate([wide if c == k else zero for c in range(count)], axis=1))
            own_keys = []
            own_values = []
            own_limits = []
            for j in range(slot_cap):
                slot = slots[r * slot_cap + j]
                safe = jnp.maximum(slot, 0)
                own_limits.append(
                    jnp.where(slot >= 0, lengths[r] - pages[base + safe] * page_size, 0)
                )
                own_keys.append(cache[safe, :page_size, :])
                own_values.append(cache[safe, page_size:, :])
            keys.append(jnp.concatenate(own_keys, axis=0))
            values.append(jnp.concatenate(own_values, axis=0))
            limits.append(own_limits)
        scores = dot_t(jnp.concatenate(wides, axis=0), jnp.concatenate(keys, axis=1))
        return scores, jnp.concatenate(values, axis=1), limits

    def weigh(scores, limits):
        all_weights = []
        stats = []
        for k in range(len(limits)):
            own = scores[k * 2 * rows : (k + 1) * 2 * rows]
            own = [
                jnp.where(
                    column < limits[k][j], own[:, j * page_size : (j + 1) * page_size], LOWEST
                )
                for j in range(slot_cap)
            ]
            peak = jnp.max(functools.reduce(jnp.maximum, own), axis=1, keepdims=True)
            peak = jnp.maximum(peak, FLOOR).astype(BF16).astype(F32)
            weights = [jnp.exp(one - peak) for one in own]
            amount = jnp.sum(functools.reduce(jnp.add, weights), axis=1, keepdims=True)
            all_weights.append(jnp.concatenate([one.astype(BF16) for one in weights], axis=1))
            stats.append((peak, amount))
        return jnp.concatenate(all_weights, axis=0), stats

    pair = 2 if requests % 2 == 0 else 1
    step = 8 if requests % 8 == 0 else pair

    def several(g, carry):
        firsts = [g * step + k for k in range(0, step, pair)]
        gathered = [gather(first, pair) for first in firsts]
        weighed = [weigh(scores, limits) for scores, _, limits in gathered]
        mixed = [dot(weighed[n][0], gathered[n][1]) for n in range(len(firsts))]
        for n, first in enumerate(firsts):
            for k in range(pair):
                own = mixed[n][k * 2 * rows : (k + 1) * 2 * rows, k * LANES : (k + 1) * LANES]
                finish(first + k, own, *weighed[n][1][k])
        return carry

    if requests == step:
        several(0, 0)
    else:
        lax.fori_loop(0, requests // step, several, 0)


def merge_kernel(arrived, tokens, gains, *refs):
    parts = arrived.shape[1]
    weights = refs[:parts]
    out, residual, columns = refs[parts:]
    part = my_part()
    for t in range(parts):
        numer, top, total = unpack_message(arrived[:, t])
        factor = jnp.exp(top - jnp.max(top, axis=0, keepdims=True))
        attended = jnp.sum(factor * numer, axis=0) / jnp.sum(factor * total, axis=0)
        columns[t] = jnp.concatenate(swap_halves(attended[0:8], attended[8:16]), axis=1)
    projected = None
    for flip in range(parts):
        one = dot(columns[part ^ flip].astype(BF16), weights[flip][...])
        projected = one if projected is None else projected + one
    rows = (tokens[part].astype(F32) + projected).astype(BF16).astype(F32)
    residual[...] = rows
    normed = normalize(rows, gains[1:2, :])
    half = normed.shape[1] // 2
    message = jnp.concatenate([normed[:, :half], normed[:, half:]], axis=0).astype(BF16)
    for n in range(out.shape[0]):
        out[n] = message


def prepare_kernel(first_far, out, near, wide, done):
    local, double, _ = near.shape
    depth = double // 2
    loads = load_all([(first_far.at[e], near.at[e]) for e in range(local)], done)

    for e in range(local):
        loads[e].wait()
        buffer = wide.at[e % 2]
        buffer[...] = near[e].astype(F32)
        out[e, :, :LANES] = buffer[pl.ds(0, depth, stride=2), :].astype(BF16)
        out[e, :, LANES:] = buffer[pl.ds(1, depth, stride=2), :].astype(BF16)


def keep_kernel(*refs):
    del refs


def names_kernel(part_rows, fresh_count, packed, out):
    requests, span, _ = packed.shape
    experts = out.shape[1]
    halves = out.shape[0] // (requests * part_rows)
    top = span // fresh_count
    row = lax.broadcasted_iota(jnp.int32, (halves * part_rows, LANES), 0)
    token = (row // part_rows) * 2 * part_rows + lax.axis_index("tp_side") * part_rows + row % part_rows
    pick = (lane_iota(row.shape) == token // fresh_count).astype(BF16)
    found = jnp.concatenate([dot_t(pick, packed[r]) for r in range(requests)], axis=0)
    fresh = lax.broadcasted_iota(jnp.int32, (found.shape[0], 1), 0) % fresh_count
    chosen = found[:, :top]
    for i in range(1, fresh_count):
        chosen = jnp.where(fresh == i, found[:, i * top : (i + 1) * top], chosen)
    lanes = lane_iota(out.shape).astype(F32)
    mask = jnp.zeros(out.shape, F32)
    for k in range(top):
        mask = jnp.where(chosen[:, k : k + 1] == lanes, 1.0, mask)
    out[...] = mask


def expert_kernel(
    copies,
    part_rows,
    group,
    arrived,
    mask,
    router,
    first,
    first_other,
    second,
    second_other,
    out,
):
    team, _, half = arrived.shape
    local = first.shape[0]
    expert_count = router.shape[0]
    count = group * part_rows
    me = lax.axis_index("req")

    def one_block(block):
        here = pl.ds(block * group, group)
        states = arrived[here].astype(F32)
        states = jnp.concatenate(
            [
                states[:, :part_rows].reshape(count, half),
                states[:, part_rows:].reshape(count, half),
            ],
            axis=1,
        ).astype(BF16)
        logits = dot_t(states, router[...])
        span = pl.ds(pl.multiple_of(block * count, count), count)
        chosen = jnp.where(mask[span, :] > 0.5, logits, LOWEST)
        shares = jnp.exp(chosen - jnp.max(chosen, axis=1, keepdims=True))
        gates = shares / jnp.sum(shares, axis=1, keepdims=True)
        lanes = lane_iota(gates.shape)
        row = lax.broadcasted_iota(jnp.int32, (count, 1), 0)
        row_request = (block * group + row // part_rows) // 2
        weights = []
        for e in range(local):
            slot = me * local + e
            gate = jnp.sum(
                jnp.where(lanes == lax.rem(slot, expert_count), gates, 0.0), axis=1, keepdims=True
            )
            if copies > 1:
                copy = lax.div(slot, expert_count)
                gate = jnp.where(lax.rem(row_request, copies) == copy, gate, 0.0)
            weights.append(gate)
        mixed = None
        for up, down in ((first, second), (first_other, second_other)):
            pieces = []
            for e in range(local):
                wide = dot(states, up[e])
                value = wide[:, :LANES]
                other = wide[:, LANES:]
                hidden = (value / (1.0 + jnp.exp(-value)) * other).astype(BF16).astype(F32)
                pieces.append((hidden * weights[e]).astype(BF16))
            part = dot(jnp.concatenate(pieces, axis=1), down[...])
            mixed = part if mixed is None else mixed + part
        out[here] = jnp.concatenate(
            [
                mixed[:, :half].reshape(group, part_rows, half),
                mixed[:, half:].reshape(group, part_rows, half),
            ],
            axis=1,
        ).astype(BF16)

    if team == group:
        one_block(0)
    else:

        def body(block, carry):
            one_block(block)
            return carry

        lax.fori_loop(0, team // group, body, 0)


def finish_kernel(arrived, residual, out):
    pairs = arrived.shape[1]
    half = arrived.shape[3]
    kept = residual[...]
    kept = jnp.concatenate([kept[:, :half], kept[:, half:]], axis=0)
    mine = lax.axis_index("tp_pair")
    for pair in range(pairs):
        mixed = jnp.sum(arrived[:, pair].astype(F32), axis=0)
        out[pair] = (mixed + jnp.where(mine == pair, kept, 0.0)).astype(BF16)


def score_kernel(fresh_count, *refs):
    *arrived, gains, weight, layer, score, ordered, wide = refs
    pairs, double, _ = arrived[0].shape
    rows = double // 2
    blocks, tokens, _ = ordered.shape
    samples = tokens // fresh_count
    side = lax.axis_index("tp_side")
    for flip in range(2):
        for pair in range(pairs):
            state = arrived[flip][pair].astype(F32)
            for other in range(flip + 2, len(arrived), 2):
                state = state + arrived[other][pair].astype(F32)
            spot = pl.ds(pl.multiple_of((2 * pair + (side ^ flip)) * rows, rows), rows)
            for c in range(blocks // 2):
                ordered[c, spot, :] = state[:rows, c * LANES : (c + 1) * LANES]
                ordered[blocks // 2 + c, spot, :] = state[rows:, c * LANES : (c + 1) * LANES]
    for c in range(blocks):
        for i in range(fresh_count):
            wide[pl.ds(fresh_count * c + i, samples, stride=fresh_count * blocks), :] = ordered[
                c, pl.ds(i, samples, stride=fresh_count), :
            ]
    layer[...] = wide[...].astype(BF16)
    states = jnp.concatenate([ordered[c] for c in range(blocks)], axis=1)
    states = states.astype(BF16).astype(F32)
    final = normalize(states, gains[2:3, :])
    scored = jnp.sum(final * weight[...], axis=1, keepdims=True)
    row = lax.broadcasted_iota(jnp.int32, (tokens, samples), 0)
    here = row // fresh_count == lane_iota(row.shape)
    for i in range(fresh_count):
        score[i : i + 1, :] = jnp.sum(
            jnp.where(here & (row % fresh_count == i), scored, 0.0), axis=0, keepdims=True
        )


def shards(
    tokens_new,
    prefix_len,
    tail_len,
    pool_home,
    pool_page,
    slot_page_cache,
    tail_cache,
    routes,
    norm_gains,
    query_weight,
    key_value_weight,
    out_weight,
    router,
    expert_in,
    expert_out,
    score_weight,
):
    req_count = lax.axis_size("req")
    pairs = lax.axis_size("tp_pair")
    parts = 2 * pairs
    _, samples, fresh_count, model = tokens_new.shape
    tokens = samples * fresh_count
    part_rows = tokens // parts
    pool = slot_page_cache.shape[0]
    page_size = slot_page_cache.shape[1]
    slot_cap = max(1, pool // req_count)
    tail_count = tail_cache.shape[2]
    local = expert_in.shape[0]
    expert_count = router.shape[1]
    copies = local * req_count // expert_count
    everyone = req_count * parts
    rows = 2 * tokens
    blocks = model // LANES
    top = routes.shape[3]
    half = model // 2
    team = req_count * pairs

    whole = ("tp_pair", "tp_side")
    flips = [[(t, t ^ flip) for t in range(parts)] for flip in range(parts)]
    first_raw = expert_in.reshape(local, 2 * model, LANES)
    second_raw = expert_out.reshape(local * LANES, model)


    token_bytes = tokens_new.reshape(samples, fresh_count, blocks, LANES)
    token_bytes = token_bytes.transpose(0, 2, 1, 3).reshape(tokens * blocks, LANES)
    route_bytes = routes[0].transpose(1, 2, 0).reshape(fresh_count * top, samples)

    message, flat, normed, cosine, sine = pl.pallas_call(
        functools.partial(query_kernel, fresh_count),
        out_shape=(
            jax.ShapeDtypeStruct((req_count, rows + fresh_count * top, LANES), BF16),
            jax.ShapeDtypeStruct((parts, part_rows, model), BF16),
            jax.ShapeDtypeStruct((tokens, model), BF16),
            jax.ShapeDtypeStruct((tokens, LANES), F32),
            jax.ShapeDtypeStruct((tokens, LANES), F32),
        ),
        in_specs=[HBM] * 6,
        out_specs=(VMEM,) * 5,
        scratch_shapes=[
            pltpu.SMEM(prefix_len.shape, jnp.int32),
            pltpu.SMEM(tail_len.shape, jnp.int32),
            pltpu.VMEM(token_bytes.shape, BF16),
            pltpu.VMEM(route_bytes.shape, jnp.int32),
            pltpu.VMEM(norm_gains.shape, F32),
            pltpu.VMEM(query_weight.shape, BF16),
            pltpu.VMEM((tokens * blocks, LANES), F32),
            pltpu.VMEM((blocks, tokens, LANES), F32),
            pltpu.SemaphoreType.DMA((6,)),
        ],
        compiler_params=params(HOLD_MIB),
        name="query",
    )(prefix_len, tail_len, token_bytes, route_bytes, norm_gains, query_weight)

    key_value_rows = key_value_weight.reshape(2 * model, LANES)
    tail_rows = tail_cache.reshape(samples, 2 * tail_count, LANES)
    tail_inputs = (message, normed, cosine, sine)
    tail = pl.pallas_call(
        functools.partial(tail_kernel, fresh_count),
        out_shape=jax.ShapeDtypeStruct((parts, 24, LANES), BF16),
        in_specs=[HBM] * 7,
        out_specs=VMEM,
        scratch_shapes=[
            pltpu.SMEM(tail_len.shape, jnp.int32),
            pltpu.VMEM((rows, LANES), BF16),
            pltpu.VMEM(normed.shape, BF16),
            pltpu.VMEM(cosine.shape, F32),
            pltpu.VMEM(sine.shape, F32),
            pltpu.VMEM(key_value_rows.shape, BF16),
            pltpu.VMEM(tail_rows.shape, BF16),
            pltpu.SemaphoreType.DMA((6,)),
            pltpu.SemaphoreType.DMA((parts,)),
        ],
        compiler_params=params(HOLD_MIB),
        cost_estimate=cost(2e9, 5e6),
        name="tail",
    )(tail_len, *tail_inputs, key_value_rows, tail_rows)

    page_rows = slot_page_cache.reshape(pool, 2 * page_size, LANES)
    later, message = lax.optimization_barrier((out_weight, message))
    across = [lax.ppermute(later, whole, flips[flip]) for flip in range(2, parts, 2)]
    beside = lax.ppermute(later, whole, flips[1])
    first_all = lax.all_to_all(message, "req", split_axis=0, concat_axis=0, tiled=True)
    page_rows, tail, beside = lax.optimization_barrier((page_rows, tail, beside))

    step = 8 if pool % 8 == 0 else 1
    split_pages = pl.pallas_call(
        split_pages_kernel,
        grid=(pool // step,),
        out_shape=jax.ShapeDtypeStruct((pool, 2 * page_size, LANES), BF16),
        in_specs=[pl.BlockSpec((step, 2 * page_size, LANES), lambda v: (v, 0, 0))],
        out_specs=pl.BlockSpec((step, 2 * page_size, LANES), lambda v: (v, 0, 0)),
        scratch_shapes=[pltpu.VMEM((step * 2 * page_size, LANES), F32)],
        compiler_params=params(8),
        cost_estimate=cost(1e6, 4e6),
        name="split_pages",
    )(page_rows)

    partial, named = pl.pallas_call(
        functools.partial(page_kernel, slot_cap),
        out_shape=(
            jax.ShapeDtypeStruct((everyone, 24, LANES), BF16),
            jax.ShapeDtypeStruct((req_count, fresh_count * top, LANES), BF16),
        ),
        in_specs=[SMEM] * 3 + [VMEM] * 3,
        out_specs=(VMEM, VMEM),
        scratch_shapes=[
            pltpu.SMEM((req_count * slot_cap,), jnp.int32),
            pltpu.SMEM((req_count,), jnp.int32),
        ],
        compiler_params=params(12),
        cost_estimate=cost(2e9, 5e6),
        name="pages",
    )(pool_home, pool_page, prefix_len, split_pages, tail, first_all)
    arrived = lax.all_to_all(partial, ("req",) + whole, split_axis=0, concat_axis=0, tiled=True)

    first_raw, across, _ = lax.optimization_barrier((first_raw, across, partial))
    projects = [out_weight, beside]
    for block in across:
        projects += [block, lax.ppermute(block, whole, flips[1])]
    first = pl.pallas_call(
        prepare_kernel,
        out_shape=jax.ShapeDtypeStruct((local, model, 2 * LANES), BF16),
        in_specs=[HBM],
        out_specs=VMEM,
        scratch_shapes=[
            pltpu.VMEM(first_raw.shape, BF16),
            pltpu.VMEM((2, 2 * model, LANES), F32),
            pltpu.SemaphoreType.DMA((local,)),
        ],
        compiler_params=params(HOLD_MIB),
        cost_estimate=cost(2e10, 8e6),
        name="prepare",
    )(first_raw)
    named, first, projects = lax.optimization_barrier((named, first, projects))
    mask = pl.pallas_call(
        functools.partial(names_kernel, part_rows, fresh_count),
        out_shape=jax.ShapeDtypeStruct((team * part_rows, expert_count), F32),
        in_specs=[VMEM],
        out_specs=VMEM,
        compiler_params=params(8),
        cost_estimate=cost(1e6, 1e6),
        name="names",
    )(named)
    arrived, first, mask = lax.optimization_barrier((arrived, first, mask))
    first = pl.pallas_call(
        keep_kernel,
        out_shape=jax.ShapeDtypeStruct(first.shape, BF16),
        in_specs=[HBM],
        out_specs=HBM,
        input_output_aliases={0: 0},
        compiler_params=params(HOLD_MIB),
        name="keep",
    )(first)
    first_other = lax.ppermute(first, whole, flips[1])

    message, residual = pl.pallas_call(
        merge_kernel,
        out_shape=(
            jax.ShapeDtypeStruct((team, 2 * part_rows, half), BF16),
            jax.ShapeDtypeStruct((part_rows, model), F32),
        ),
        in_specs=[VMEM] * (3 + parts),
        out_specs=(VMEM, VMEM),
        scratch_shapes=[pltpu.VMEM((parts, part_rows, model // parts), F32)],
        compiler_params=params(12),
        name="merge",
    )(arrived.reshape(req_count, parts, 24, LANES), flat, norm_gains, *projects)
    message, second_sent = lax.optimization_barrier((message, second_raw))
    second_other = lax.ppermute(second_sent, whole, flips[1])
    states = lax.all_to_all(message, ("req", "tp_pair"), split_axis=0, concat_axis=0, tiled=True)

    expert_inputs = (
        states,
        mask,
        router.T,
        first,
        first_other,
        second_raw,
        second_other,
    )
    mixed = pl.pallas_call(
        functools.partial(expert_kernel, copies, part_rows, min(req_count, 8) * pairs),
        out_shape=jax.ShapeDtypeStruct((team, 2 * part_rows, half), BF16),
        in_specs=[VMEM] * 7,
        out_specs=VMEM,
        compiler_params=params(16),
        name="experts",
    )(*expert_inputs)
    mixed = mixed.reshape(req_count, pairs, 2 * part_rows, half)
    mixed = lax.all_to_all(mixed, "req", split_axis=0, concat_axis=0, tiled=True)

    finished = pl.pallas_call(
        finish_kernel,
        out_shape=jax.ShapeDtypeStruct((pairs, 2 * part_rows, half), BF16),
        in_specs=[VMEM, VMEM],
        out_specs=VMEM,
        compiler_params=params(8),
        name="finish",
    )(mixed, residual)
    gathered = [finished] + [
        lax.ppermute(finished, whole, flips[flip]) for flip in range(1, parts)
    ]

    layer, score = pl.pallas_call(
        functools.partial(score_kernel, fresh_count),
        out_shape=(
            jax.ShapeDtypeStruct((tokens * blocks, LANES), BF16),
            jax.ShapeDtypeStruct((fresh_count, samples), F32),
        ),
        in_specs=[VMEM] * (parts + 2),
        out_specs=(VMEM, VMEM),
        scratch_shapes=[
            pltpu.VMEM((blocks, tokens, LANES), F32),
            pltpu.VMEM((tokens * blocks, LANES), F32),
        ],
        compiler_params=params(8),
        name="score",
    )(*gathered, norm_gains, score_weight.reshape(1, model))
    layer = layer.reshape(samples, blocks, fresh_count, LANES).transpose(0, 2, 1, 3)
    return (
        layer.reshape(1, samples, fresh_count, model),
        score.T.reshape(1, samples, fresh_count),
    )


def solution(mesh):
    tp = ("tp_pair", "tp_side")
    req_count, parts = mesh.devices.shape
    mesh = jax.sharding.Mesh(
        mesh.devices.reshape(req_count, parts // 2, 2), ("req", "tp_pair", "tp_side")
    )
    placed = (
        P("req", None, None, None),
        P(),
        P("req", None),
        P(),
        P(),
        P("req", None, None, tp),
        P("req", None, None, None, tp),
        P("req", None, None, None),
        P(),
        P(None, tp),
        P(None, None, tp),
        P(tp, None),
        P(),
        P("req", None, None, tp),
        P("req", tp, None),
        P(),
    )
    return jax.shard_map(
        shards,
        mesh=mesh,
        in_specs=placed,
        out_specs=(P("req", None, None, None), P("req", None, None)),
        check_vma=False,
    )
```

profile of v0, /device:TPU:0, one launch (start us, length us, event | category | flops | bytes accessed | tf_op | source)
XLA Modules:
  0.0 68.4 jit_solution(17780750340420160579)
XLA Ops:
  0.6 2.3 %query.1 = (bf16[8,80,128]{2,1,0:T(8,128)(2,1)}, bf16[4,8,1024]{2,1,0:T(8,128)(2,1)}, bf16[32,1024]{1,0:T(8,128)(2,1)}, f32[32,128]{1,0:T(8,128)}, f32[32,128]{1,0:T(8,128)}) custom-call(s32[8]{0:T(128)} %lengths.1, s32[1,16]{1,0:T(1,128)} %lengths_far.3, bf16[256,128]{1,0:T(8,128)(2,1)} %bitcast.34, s32[16,16]{1,0:T(8,128)} %bitcast.35, f32[3,1024]{1,0:T(4,128)} %refs_4_.1, ...), custom_call_target="tpu_custom_call" | custom-call | tf_op jit(solution)/shard_map/query/pallas_call | solution.py:652
  2.9 0.5 collective-permute-start
  3.4 2.6 %collective-permute-start.1 = (bf16[256,1024]{1,0:T(8,128)(2,1)}, bf16[256,1024]{1,0:T(8,128)(2,1)S(1)}, u32[]{:S(2)}, u32[]{:S(2)}) collective-permute-start(bf16[256,1024]{1,0:T(8,128)(2,1)} %refs_0_), channel_id=1, source_target_pairs={{0,2},{1,3},{2,0},{3,1},{4,6},{5,7},{6,4},{7,5},{8,10},{9,11},{10,... | collective-permute-start | bytes 1572872 | tf_op jit(solution)/shard_map/ppermute | solution.py:704
  6.0 5.8 %all-to-all-start = ((bf16[8,80,128]{2,1,0:T(8,128)(2,1)}), bf16[8,80,128]{2,1,0:T(8,128)(2,1)S(1)}, u32[]{:S(2)}, u32[]{:S(2)}) async-start(bf16[8,80,128]{2,1,0:T(8,128)(2,1)} %get-tuple-element.38.query_far), calls=%async_computation | async-start | bytes 327680 | tf_op jit(solution)/shard_map/all_to_all | solution.py:706
  11.8 5.4 %tail.1 = bf16[4,24,128]{2,1,0:T(8,128)(2,1)} custom-call(s32[1,16]{1,0:T(1,128)} %lengths_far.3, bf16[8,80,128]{2,1,0:T(8,128)(2,1)} %get-tuple-element.38.query_far, bf16[32,1024]{1,0:T(8,128)(2,1)} %get-tuple-element.32.normed_far, f32[32,128]{1,0:T(8,128)} %get-tuple-element.33.cosine_far, f32[32,128]{1,0:T(8,128)} %get-tuple-element.34.sine_far, ...), custom_call_target="tpu_custom_call" | custom-call | flops 2000000000 | bytes 5000000 | tf_op jit(solution)/shard_map/tail/pallas_call | solution.py:681
  17.3 0.6 split_pages.1.cache
  17.8 1.8 %all-to-all-done.query = bf16[8,80,128]{2,1,0:T(8,128)(2,1)S(1)} async-done(((bf16[8,80,128]{2,1,0:T(8,128)(2,1)}), bf16[8,80,128]{2,1,0:T(8,128)(2,1)S(1)}, u32[]{:S(2)}, u32[]{:S(2)}) %all-to-all-start) | async-done | bytes 163872 | tf_op jit(solution)/shard_map/all_to_all | solution.py:706
  19.6 2.9 %pages.2 = (bf16[32,24,128]{2,1,0:T(8,128)(2,1)}, bf16[8,16,128]{2,1,0:T(8,128)(2,1)S(1)}) custom-call(s32[256]{0:T(256)S(1)} %copy-done.9, s32[256]{0:T(256)S(1)} %copy-done.10, s32[8]{0:T(128)S(1)} %copy-done.8, bf16[32,256,128]{2,1,0:T(8,128)(2,1)S(1)} %split_pages.1.cache, bf16[4,24,128]{2,1,0:T(8,128)(2,1)S(1)} %copy-done.11, ...), custom_call_target="tpu_custom_call" | custom-call | flops 2000000000 | bytes 5000000 | tf_op jit(solution)/shard_map/pages/pallas_call | solution.py:722
  22.5 3.5 %all-to-all-start.1 = ((bf16[32,24,128]{2,1,0:T(8,128)(2,1)}), bf16[32,24,128]{2,1,0:T(8,128)(2,1)S(1)}, u32[]{:S(2)}, u32[]{:S(2)}) async-start(bf16[32,24,128]{2,1,0:T(8,128)(2,1)} %get-tuple-element.39), calls=%async_computation.1 | async-start | bytes 393216 | tf_op jit(solution)/shard_map/all_to_all | solution.py:738
  26.0 0.3 collective-permute-start.2
  26.3 3.0 %prepare.1.refs_0_ = bf16[4,1024,256]{2,1,0:T(8,128)(2,1)} custom-call(bf16[4,2048,128]{2,1,0:T(8,128)(2,1)} %bitcast.37), custom_call_target="tpu_custom_call" | custom-call | flops 20000000000 | bytes 8000000 | tf_op jit(solution)/shard_map/prepare/pallas_call | solution.py:744
  29.4 0.4 names.1.mask
  29.9 5.0 %all-to-all-done.1 = bf16[32,24,128]{2,1,0:T(8,128)(2,1)S(1)} async-done(((bf16[32,24,128]{2,1,0:T(8,128)(2,1)}), bf16[32,24,128]{2,1,0:T(8,128)(2,1)S(1)}, u32[]{:S(2)}, u32[]{:S(2)}) %all-to-all-start.1) | async-done | bytes 196640 | tf_op jit(solution)/shard_map/all_to_all | solution.py:738
  34.9 0.7 collective-permute-start.3
  35.6 1.0 %merge.1 = (bf16[16,16,512]{2,1,0:T(8,128)(2,1)S(1)}, f32[8,1024]{1,0:T(8,128)S(1)}) custom-call(bf16[8,4,24,128]{3,2,1,0:T(8,128)(2,1)S(1)} %bitcast.31, bf16[4,8,1024]{2,1,0:T(8,128)(2,1)S(1)} %copy-done.6, f32[3,1024]{1,0:T(4,128)S(1)} %copy-done.4, bf16[256,1024]{1,0:T(8,128)(2,1)S(1)} %copy-done.3, bf16[256,1024]{1,0:T(8,128)(2,1)S(1)} %collective-permute-done.refs_1_, ...), custom_call_target="tpu_custom_call" | custom-call | tf_op jit(solution)/shard_map/merge/pallas_call | solution.py:780
  36.5 0.2 collective-permute-start.4
  36.7 13.5 %all_to_all.20.arrived = bf16[16,16,512]{2,1,0:T(8,128)(2,1)S(1)} all-to-all(bf16[16,16,512]{2,1,0:T(8,128)(2,1)S(1)} %get-tuple-element.53), channel_id=1, replica_groups=mesh['req'=8,'tp_pair'=2,'tp_side'=2] {'req','tp_pair'}, dimensions={0} | all-to-all | bytes 524288 | tf_op jit(solution)/shard_map/all_to_all | solution.py:794
  50.2 1.4 %experts.1 = bf16[16,16,512]{2,1,0:T(8,128)(2,1)S(1)} custom-call(bf16[16,16,512]{2,1,0:T(8,128)(2,1)S(1)} %all_to_all.20.arrived, f32[128,32]{1,0:T(8,128)S(1)} %names.1.mask, bf16[32,1024]{1,0:T(8,128)(2,1)S(1)} %bitcast.32, bf16[4,1024,256]{2,1,0:T(8,128)(2,1)S(1)} %copy-done, bf16[4,1024,256]{2,1,0:T(8,128)(2,1)S(1)} %collective-permute-done.3.first_other, ...), custom_call_target="tpu_custom_call" | custom-call | tf_op jit(solution)/shard_map/experts/pallas_call | solution.py:805
  51.6 11.8 %all_to_all.21.arrived = bf16[8,2,16,512]{3,2,1,0:T(8,128)(2,1)S(1)} all-to-all(bf16[8,2,16,512]{3,2,1,0:T(8,128)(2,1)S(1)} %bitcast.30), channel_id=1, replica_groups=mesh['req'=8,'tp_pair'=2,'tp_side'=2] {'req'}, dimensions={0} | all-to-all | bytes 524288 | tf_op jit(solution)/shard_map/all_to_all | solution.py:814
  63.5 0.6 collective-permute-start.6
  64.2 1.2 %collective-permute-start.5 = (bf16[2,16,512]{2,1,0:T(8,128)(2,1)S(1)}, bf16[2,16,512]{2,1,0:T(8,128)(2,1)S(1)}, u32[]{:S(2)}, u32[]{:S(2)}) collective-permute-start(bf16[2,16,512]{2,1,0:T(8,128)(2,1)S(1)} %finish.1.refs_0_), channel_id=1, source_target_pairs={{0,1},{1,0},{2,3},{3,2},{4,5},{5,4},{6,7},{7,6},{8,9},{9,8},{10,11... | collective-permute-start | bytes 98312 | tf_op jit(solution)/shard_map/ppermute | solution.py:825
  65.4 1.5 %collective-permute-done.7.refs_3_ = bf16[2,16,512]{2,1,0:T(8,128)(2,1)S(1)} collective-permute-done((bf16[2,16,512]{2,1,0:T(8,128)(2,1)S(1)}, bf16[2,16,512]{2,1,0:T(8,128)(2,1)S(1)}, u32[]{:S(2)}, u32[]{:S(2)}) %collective-permute-start.7) | collective-permute-done | bytes 32800 | tf_op jit(solution)/shard_map/ppermute | solution.py:825
  66.9 0.7 %collective-permute-done.6.refs_2_ = bf16[2,16,512]{2,1,0:T(8,128)(2,1)S(1)} collective-permute-done((bf16[2,16,512]{2,1,0:T(8,128)(2,1)S(1)}, bf16[2,16,512]{2,1,0:T(8,128)(2,1)S(1)}, u32[]{:S(2)}, u32[]{:S(2)}) %collective-permute-start.6) | collective-permute-done | bytes 32800 | tf_op jit(solution)/shard_map/ppermute | solution.py:825
  67.6 0.8 %score.1 = (bf16[256,128]{1,0:T(8,128)(2,1)}, f32[2,16]{1,0:T(2,128)}) custom-call(bf16[2,16,512]{2,1,0:T(8,128)(2,1)S(1)} %finish.1.refs_0_, bf16[2,16,512]{2,1,0:T(8,128)(2,1)S(1)} %collective-permute-done.5.refs_1_, bf16[2,16,512]{2,1,0:T(8,128)(2,1)S(1)} %collective-permute-done.6.refs_2_, bf16[2,16,512]{2,1,0:T(8,128)(2,1)S(1)} %collective-permute-done.7.refs_3_, ...), custom_call_target="tpu_custom_call" | custom-call | tf_op jit(solution)/shard_map/score/pallas_call | solution.py:828
  (33 shorter events, 0.2 us)
Async XLA Ops:
  2.9 14.3 %collective-permute-start = (bf16[256,1024]{1,0:T(8,128)(2,1)}, bf16[256,1024]{1,0:T(8,128)(2,1)S(1)}, u32[]{:S(2)}, u32[]{:S(2)}) collective-permute-start(bf16[256,1024]{1,0:T(8,128)(2,1)} %refs_0_), channel_id=1, source_target_pairs={{0,1},{1,0},{2,3},{3,2},{4,5},{5,4},{6,7},{7,6},{8,9},{9,8},{10,11... | collective-permute-start | bytes 1572872 | tf_op jit(solution)/shard_map/ppermute | solution.py:705
  3.4 22.6 %collective-permute-start.1 = (bf16[256,1024]{1,0:T(8,128)(2,1)}, bf16[256,1024]{1,0:T(8,128)(2,1)S(1)}, u32[]{:S(2)}, u32[]{:S(2)}) collective-permute-start(bf16[256,1024]{1,0:T(8,128)(2,1)} %refs_0_), channel_id=1, source_target_pairs={{0,2},{1,3},{2,0},{3,1},{4,6},{5,7},{6,4},{7,5},{8,10},{9,11},{10,... | collective-permute-start | bytes 1572872 | tf_op jit(solution)/shard_map/ppermute | solution.py:704
  6.0 13.6 %all-to-all-start = ((bf16[8,80,128]{2,1,0:T(8,128)(2,1)}), bf16[8,80,128]{2,1,0:T(8,128)(2,1)S(1)}, u32[]{:S(2)}, u32[]{:S(2)}) async-start(bf16[8,80,128]{2,1,0:T(8,128)(2,1)} %get-tuple-element.38.query_far), calls=%async_computation | async-start | bytes 327680 | tf_op jit(solution)/shard_map/all_to_all | solution.py:706
  11.8 5.4 %copy-start.1 = (bf16[32,128,2,128]{3,2,1,0:T(2,128)(2,1)S(1)}, bf16[32,128,2,128]{3,2,1,0:T(2,128)(2,1)}, u32[]{:S(2)}) copy-start(bf16[32,128,2,128]{3,2,1,0:T(2,128)(2,1)} %param.21) | copy-start | bytes 6291460
  17.2 2.4 %copy-start.8 = (s32[8]{0:T(128)S(1)}, s32[8]{0:T(128)}, u32[]{:S(2)}) copy-start(s32[8]{0:T(128)} %lengths.1) | copy-start | bytes 100
  17.2 2.4 %copy-start.9 = (s32[256]{0:T(256)S(1)}, s32[256]{0:T(256)}, u32[]{:S(2)}) copy-start(s32[256]{0:T(256)} %homes.1) | copy-start | bytes 3076
  17.3 2.4 %copy-start.10 = (s32[256]{0:T(256)S(1)}, s32[256]{0:T(256)}, u32[]{:S(2)}) copy-start(s32[256]{0:T(256)} %pages.3) | copy-start | bytes 3076
  17.3 2.4 %copy-start.11 = (bf16[4,24,128]{2,1,0:T(8,128)(2,1)S(1)}, bf16[4,24,128]{2,1,0:T(8,128)(2,1)}, u32[]{:S(2)}) copy-start(bf16[4,24,128]{2,1,0:T(8,128)(2,1)} %tail.1) | copy-start | bytes 73732
  22.5 12.4 %all-to-all-start.1 = ((bf16[32,24,128]{2,1,0:T(8,128)(2,1)}), bf16[32,24,128]{2,1,0:T(8,128)(2,1)S(1)}, u32[]{:S(2)}, u32[]{:S(2)}) async-start(bf16[32,24,128]{2,1,0:T(8,128)(2,1)} %get-tuple-element.39), calls=%async_computation.1 | async-start | bytes 393216 | tf_op jit(solution)/shard_map/all_to_all | solution.py:738
  26.0 3.4 %collective-permute-start.2 = (bf16[256,1024]{1,0:T(8,128)(2,1)S(1)}, bf16[256,1024]{1,0:T(8,128)(2,1)S(1)}, u32[]{:S(2)}, u32[]{:S(2)}) collective-permute-start(bf16[256,1024]{1,0:T(8,128)(2,1)S(1)} %collective-permute-done.1.refs_2_), channel_id=1, source_target_pairs={{0,1},{1,0},{2,3},{3,2},{4,5},{5,4},{6,7},{7,6},{8,9},{9,8},{10,11... | collective-permute-start | bytes 1572872 | tf_op jit(solution)/shard_map/ppermute | solution.py:743
  29.8 5.7 %copy-start.3 = (bf16[256,1024]{1,0:T(8,128)(2,1)S(1)}, bf16[256,1024]{1,0:T(8,128)(2,1)}, u32[]{:S(2)}) copy-start(bf16[256,1024]{1,0:T(8,128)(2,1)} %refs_0_) | copy-start | bytes 1572868
  29.8 5.7 %copy-start.4 = (f32[3,1024]{1,0:T(4,128)S(1)}, f32[3,1024]{1,0:T(4,128)}, u32[]{:S(2)}) copy-start(f32[3,1024]{1,0:T(4,128)} %refs_4_.1) | copy-start | bytes 36868
  29.8 5.7 %copy-start.6 = (bf16[4,8,1024]{2,1,0:T(8,128)(2,1)S(1)}, bf16[4,8,1024]{2,1,0:T(8,128)(2,1)}, u32[]{:S(2)}) copy-start(bf16[4,8,1024]{2,1,0:T(8,128)(2,1)} %get-tuple-element.47.tokens) | copy-start | bytes 196612
  34.9 1.6 %copy-start.2 = (bf16[4,128,1024]{2,1,0:T(8,128)(2,1)S(1)}, bf16[4,128,1024]{2,1,0:T(8,128)(2,1)}, u32[]{:S(2)}) copy-start(bf16[4,128,1024]{2,1,0:T(8,128)(2,1)} %param.30) | copy-start | bytes 3145732
  34.9 15.3 %copy-start = (bf16[4,1024,256]{2,1,0:T(8,128)(2,1)S(1)}, bf16[4,1024,256]{2,1,0:T(8,128)(2,1)}, u32[]{:S(2)}) copy-start(bf16[4,1024,256]{2,1,0:T(8,128)(2,1)} %keep.1.first) | copy-start | bytes 6291460
  34.9 15.3 %copy-start.5 = (bf16[1024,32]{0,1:T(8,128)(2,1)S(1)}, bf16[1024,32]{0,1:T(8,128)(2,1)}, u32[]{:S(2)}) copy-start(bf16[1024,32]{0,1:T(8,128)(2,1)} %param.28) | copy-start | bytes 196612
  34.9 15.3 %collective-permute-start.3 = (bf16[4,1024,256]{2,1,0:T(8,128)(2,1)}, bf16[4,1024,256]{2,1,0:T(8,128)(2,1)S(1)}, u32[]{:S(2)}, u32[]{:S(2)}) collective-permute-start(bf16[4,1024,256]{2,1,0:T(8,128)(2,1)} %keep.1.first), channel_id=1, source_target_pairs={{0,1},{1,0},{2,3},{3,2},{4,5},{5,4},{6,7},{7,6},{8,9},{9,8},{10,11... | collective-permute-start | bytes 6291464 | tf_op jit(solution)/shard_map/ppermute | solution.py:778
  36.5 13.6 %collective-permute-start.4 = (bf16[512,1024]{1,0:T(8,128)(2,1)S(1)}, bf16[512,1024]{1,0:T(8,128)(2,1)S(1)}, u32[]{:S(2)}, u32[]{:S(2)}) collective-permute-start(bf16[512,1024]{1,0:T(8,128)(2,1)S(1)} %bitcast.28), channel_id=1, source_target_pairs={{0,1},{1,0},{2,3},{3,2},{4,5},{5,4},{6,7},{7,6},{8,9},{9,8},{10,11... | collective-permute-start | bytes 3145736 | tf_op jit(solution)/shard_map/ppermute | solution.py:793
  50.2 17.4 %copy-start.7 = (f32[1024]{0:T(1024)S(1)}, f32[1024]{0:T(1024)}, u32[]{:S(2)}) copy-start(f32[1024]{0:T(1024)} %param.31) | copy-start | bytes 12292
  63.4 3.4 %collective-permute-start.7 = (bf16[2,16,512]{2,1,0:T(8,128)(2,1)S(1)}, bf16[2,16,512]{2,1,0:T(8,128)(2,1)S(1)}, u32[]{:S(2)}, u32[]{:S(2)}) collective-permute-start(bf16[2,16,512]{2,1,0:T(8,128)(2,1)S(1)} %finish.1.refs_0_), channel_id=1, source_target_pairs={{0,3},{1,2},{2,1},{3,0},{4,7},{5,6},{6,5},{7,4},{8,11},{9,10},{10,... | collective-permute-start | bytes 98312 | tf_op jit(solution)/shard_map/ppermute | solution.py:825
  63.5 4.0 %collective-permute-start.6 = (bf16[2,16,512]{2,1,0:T(8,128)(2,1)S(1)}, bf16[2,16,512]{2,1,0:T(8,128)(2,1)S(1)}, u32[]{:S(2)}, u32[]{:S(2)}) collective-permute-start(bf16[2,16,512]{2,1,0:T(8,128)(2,1)S(1)} %finish.1.refs_0_), channel_id=1, source_target_pairs={{0,2},{1,3},{2,0},{3,1},{4,6},{5,7},{6,4},{7,5},{8,10},{9,11},{10,... | collective-permute-start | bytes 98312 | tf_op jit(solution)/shard_map/ppermute | solution.py:825
  64.2 3.4 %collective-permute-start.5 = (bf16[2,16,512]{2,1,0:T(8,128)(2,1)S(1)}, bf16[2,16,512]{2,1,0:T(8,128)(2,1)S(1)}, u32[]{:S(2)}, u32[]{:S(2)}) collective-permute-start(bf16[2,16,512]{2,1,0:T(8,128)(2,1)S(1)} %finish.1.refs_0_), channel_id=1, source_target_pairs={{0,1},{1,0},{2,3},{3,2},{4,5},{5,4},{6,7},{7,6},{8,9},{9,8},{10,11... | collective-permute-start | bytes 98312 | tf_op jit(solution)/shard_map/ppermute | solution.py:825
where the time goes:
time: 68.8 us; the launch traced here: 68.4 us
  blocking collectives  25.2 us (37%)
  Pallas kernels  17.8 us (26%)
  starting transfers between devices  15.4 us (22%)
  waiting for transfers between devices  9.01 us (13%)
  between operations  0.85 us (1%)
    all_to_all x1, blocking collectives, shards(): lax.all_to_all(message, ('req', 'tp_pair'), split_axis=0, concat_axis=0,...  13.5 us
    all_to_all x1, blocking collectives, shards(): lax.all_to_all(mixed, 'req', split_axis=0, concat_axis=0, tiled=True)  11.8 us
    all_to_all x1, starting transfers between devices, shards(): lax.all_to_all(message, 'req', split_axis=0, concat_axis=0, tiled=True)  5.81 us
    pallas_call x1, Pallas kernels, shards(): pl.pallas_call(functools.partial(tail_kernel, fresh_count), out_shape=jax...  5.38 us
    all_to_all x1, waiting for transfers between devices, shards(): lax.all_to_all(partial, ('req',) + whole, split_axis=0, concat_axis=0, ti...  5.04 us
    all_to_all x1, starting transfers between devices, shards(): lax.all_to_all(partial, ('req',) + whole, split_axis=0, concat_axis=0, ti...  3.46 us
    pallas_call x1, Pallas kernels, shards(): pl.pallas_call(prepare_kernel, out_shape=jax.ShapeDtypeStruct((local, mod...  3.03 us
    pallas_call x1, Pallas kernels, shards(): pl.pallas_call(functools.partial(page_kernel, slot_cap), out_shape=(jax.S...  2.9 us
  transfers between devices with their start and end apart: 10, of which 4 were waited for; matrix products, arithmetic and copies ran while one was open for 0% of the time, Pallas kernels for 19%

commit v1 on v0

--- a/solution.py
+++ b/solution.py
@@ -160,8 +160,7 @@
         )
     )
     packed = jnp.concatenate(packed, axis=0).astype(BF16)
-    for n in range(message.shape[0]):
-        message[n] = packed
+    message[...] = packed
 
 
 def split_pages_kernel(source, out, wide):
@@ -231,7 +230,7 @@
             (weight_far, weight),
             (cosine_far, cosine),
             (sine_far, sine),
-            (query_far.at[0, pl.ds(0, parts * 16)], query),
+            (query_far.at[pl.ds(0, parts * 16)], query),
             (lengths_far, lengths),
         ),
         load,
@@ -306,9 +305,16 @@
         )
 
 
+def stack_kernel(*refs):
+    *blocks, out = refs
+    for k, block in enumerate(blocks):
+        out[k] = block[...]
+
+
 def page_kernel(
-    slot_cap, homes, pages, lengths, cache, tail, query, out, named, slots, counts
+    slot_cap, homes, pages, lengths, cache, tail, *refs
 ):
+    *blocks, out, named, query, slots, counts = refs
     requests = query.shape[0]
     parts = tail.shape[0]
     pool = cache.shape[0]
@@ -319,6 +325,12 @@
     tail_numer, tail_top, tail_total = [
         kind.reshape(rows, LANES) for kind in unpack_message(tail[...])
     ]
+    if len(blocks) == 1:
+        query[...] = blocks[0][...]
+    else:
+        for n, block in enumerate(blocks):
+            for k in range(block.shape[0]):
+                query[me ^ (block.shape[0] * n + k)] = block[k]
     named[...] = query[:, rows:, :]
 
     def clear(r, carry):
@@ -652,7 +664,7 @@
     message, flat, normed, cosine, sine = pl.pallas_call(
         functools.partial(query_kernel, fresh_count),
         out_shape=(
-            jax.ShapeDtypeStruct((req_count, rows + fresh_count * top, LANES), BF16),
+            jax.ShapeDtypeStruct((rows + fresh_count * top, LANES), BF16),
             jax.ShapeDtypeStruct((parts, part_rows, model), BF16),
             jax.ShapeDtypeStruct((tokens, model), BF16),
             jax.ShapeDtypeStruct((tokens, LANES), F32),
@@ -677,6 +689,44 @@
 
     key_value_rows = key_value_weight.reshape(2 * model, LANES)
     tail_rows = tail_cache.reshape(samples, 2 * tail_count, LANES)
+    page_rows = slot_page_cache.reshape(pool, 2 * page_size, LANES)
+    later, message = lax.optimization_barrier((out_weight, message))
+    across = [lax.ppermute(later, whole, flips[flip]) for flip in range(2, parts, 2)]
+    beside = lax.ppermute(later, whole, flips[1])
+    if req_count == 8:
+        xor = [[(d, d ^ flip) for d in range(req_count)] for flip in range(req_count)]
+        near = lax.ppermute(message, "req", xor[1])
+        page_rows, message = lax.optimization_barrier((page_rows, message))
+    step = 8 if pool % 8 == 0 else 1
+    split_pages = pl.pallas_call(
+        split_pages_kernel,
+        grid=(pool // step,),
+        out_shape=jax.ShapeDtypeStruct((pool, 2 * page_size, LANES), BF16),
+        in_specs=[pl.BlockSpec((step, 2 * page_size, LANES), lambda v: (v, 0, 0))],
+        out_specs=pl.BlockSpec((step, 2 * page_size, LANES), lambda v: (v, 0, 0)),
+        scratch_shapes=[pltpu.VMEM((step * 2 * page_size, LANES), F32)],
+        compiler_params=params(8),
+        cost_estimate=cost(1e6, 4e6),
+        name="split_pages",
+    )(page_rows)
+
+    if req_count == 8:
+        split_pages, near = lax.optimization_barrier((split_pages, near))
+        stacked = pl.pallas_call(
+            stack_kernel,
+            out_shape=jax.ShapeDtypeStruct((2,) + message.shape, BF16),
+            in_specs=[VMEM] * 2,
+            out_specs=VMEM,
+            compiler_params=params(8),
+            name="stack",
+        )(message, near)
+        normed, stacked = lax.optimization_barrier((normed, stacked))
+        first_all = [stacked] + [lax.ppermute(stacked, "req", xor[flip]) for flip in (2, 4, 6)]
+    else:
+        copies_out = jnp.broadcast_to(message[None], (req_count,) + message.shape)
+        first_all = [
+            lax.all_to_all(copies_out, "req", split_axis=0, concat_axis=0, tiled=True)
+        ]
     tail_inputs = (message, normed, cosine, sine)
     tail = pl.pallas_call(
         functools.partial(tail_kernel, fresh_count),
@@ -699,25 +749,7 @@
         name="tail",
     )(tail_len, *tail_inputs, key_value_rows, tail_rows)
 
-    page_rows = slot_page_cache.reshape(pool, 2 * page_size, LANES)
-    later, message = lax.optimization_barrier((out_weight, message))
-    across = [lax.ppermute(later, whole, flips[flip]) for flip in range(2, parts, 2)]
-    beside = lax.ppermute(later, whole, flips[1])
-    first_all = lax.all_to_all(message, "req", split_axis=0, concat_axis=0, tiled=True)
-    page_rows, tail, beside = lax.optimization_barrier((page_rows, tail, beside))
-
-    step = 8 if pool % 8 == 0 else 1
-    split_pages = pl.pallas_call(
-        split_pages_kernel,
-        grid=(pool // step,),
-        out_shape=jax.ShapeDtypeStruct((pool, 2 * page_size, LANES), BF16),
-        in_specs=[pl.BlockSpec((step, 2 * page_size, LANES), lambda v: (v, 0, 0))],
-        out_specs=pl.BlockSpec((step, 2 * page_size, LANES), lambda v: (v, 0, 0)),
-        scratch_shapes=[pltpu.VMEM((step * 2 * page_size, LANES), F32)],
-        compiler_params=params(8),
-        cost_estimate=cost(1e6, 4e6),
-        name="split_pages",
-    )(page_rows)
+    split_pages, beside, tail = lax.optimization_barrier((split_pages, beside, tail))
 
     partial, named = pl.pallas_call(
         functools.partial(page_kernel, slot_cap),
@@ -725,16 +757,17 @@
             jax.ShapeDtypeStruct((everyone, 24, LANES), BF16),
             jax.ShapeDtypeStruct((req_count, fresh_count * top, LANES), BF16),
         ),
-        in_specs=[SMEM] * 3 + [VMEM] * 3,
+        in_specs=[SMEM] * 3 + [VMEM] * (2 + len(first_all)),
         out_specs=(VMEM, VMEM),
         scratch_shapes=[
+            pltpu.VMEM((req_count,) + message.shape, BF16),
             pltpu.SMEM((req_count * slot_cap,), jnp.int32),
             pltpu.SMEM((req_count,), jnp.int32),
         ],
         compiler_params=params(12),
         cost_estimate=cost(2e9, 5e6),
         name="pages",
-    )(pool_home, pool_page, prefix_len, split_pages, tail, first_all)
+    )(pool_home, pool_page, prefix_len, split_pages, tail, *first_all)
     arrived = lax.all_to_all(partial, ("req",) + whole, split_axis=0, concat_axis=0, tiled=True)
 
     first_raw, across, _ = lax.optimization_barrier((first_raw, across, partial))

time: 68.8 us -> 71 us (1.032)
  local copies, waits for them, and re-layouts: 0.06 us -> 2.37 us
  starting transfers between devices: 15.4 us -> 16.9 us
  waiting for transfers between devices: 9.01 us -> 7.59 us
    ppermute x0 -> x4, starting transfers between devices: none -> 5.88 us  [the longest x3 4.39 us: shards(): lax.ppermute(stacked, 'req', xor[flip])]
    all_to_all x1 -> x0, starting transfers between devices: 5.81 us -> none  [shards(): lax.all_to_all(message, 'req', split_axis=0, concat_axis=0, tiled=True)]
    unnamed x24 -> x26, local copies, waits for them, and re-layouts: 0.06 us -> 2.37 us
    all_to_all x1 -> x0, waiting for transfers between devices: 1.77 us -> none  [shards(): lax.all_to_all(message, 'req', split_axis=0, concat_axis=0, tiled=True)]
    all_to_all x1, starting transfers between devices: 3.46 us -> 4.89 us  [shards(): lax.all_to_all(partial, ('req',) + whole, split_axis=0, concat_axis=0, ti...]
  transfers between devices with their start and end apart: 10 -> 13, of which waited for: 4 -> 4; matrix products, arithmetic and copies ran while one was open for 0% -> 0% of each run, Pallas kernels for 19% -> 19%
where the time goes in v1:
time: 71 us; the launch traced here: 70.6 us
  blocking collectives  25.2 us (35%)
  Pallas kernels  17.6 us (25%)
  starting transfers between devices  16.9 us (24%)
  waiting for transfers between devices  7.59 us (11%)
  local copies, waits for them, and re-layouts  2.37 us (3%)
  between operations  0.85 us (1%)
    all_to_all x1, blocking collectives, shards(): lax.all_to_all(message, ('req', 'tp_pair'), split_axis=0, concat_axis=0,...  13.5 us
    all_to_all x1, blocking collectives, shards(): lax.all_to_all(mixed, 'req', split_axis=0, concat_axis=0, tiled=True)  11.8 us
    pallas_call x1, Pallas kernels, shards(): pl.pallas_call(functools.partial(tail_kernel, fresh_count), out_shape=jax...  5.28 us
    all_to_all x1, waiting for transfers between devices, shards(): lax.all_to_all(partial, ('req',) + whole, split_axis=0, concat_axis=0, ti...  5.02 us
    all_to_all x1, starting transfers between devices, shards(): lax.all_to_all(partial, ('req',) + whole, split_axis=0, concat_axis=0, ti...  4.89 us
    ppermute x3, starting transfers between devices, shards(): lax.ppermute(stacked, 'req', xor[flip])  4.39 us
    pallas_call x1, Pallas kernels, shards(): pl.pallas_call(prepare_kernel, out_shape=jax.ShapeDtypeStruct((local, mod...  3.05 us
    pallas_call x1, Pallas kernels, shards(): pl.pallas_call(functools.partial(page_kernel, slot_cap), out_shape=(jax.S...  2.9 us
  transfers between devices with their start and end apart: 13, of which 4 were waited for; matrix products, arithmetic and copies ran while one was open for 0% of the time, Pallas kernels for 19%

profile of v1, /device:TPU:0, one launch (start us, length us, event | category | flops | bytes accessed | tf_op | source)
XLA Modules:
  0.0 70.6 jit_solution(3422125970535460607)
XLA Ops:
  0.6 2.2 %query.1 = (bf16[80,128]{1,0:T(8,128)(2,1)}, bf16[4,8,1024]{2,1,0:T(8,128)(2,1)}, bf16[32,1024]{1,0:T(8,128)(2,1)}, f32[32,128]{1,0:T(8,128)}, f32[32,128]{1,0:T(8,128)}) custom-call(s32[8]{0:T(128)} %lengths.1, s32[1,16]{1,0:T(1,128)} %lengths_far.3, bf16[256,128]{1,0:T(8,128)(2,1)} %bitcast.34, s32[16,16]{1,0:T(8,128)} %bitcast.35, f32[3,1024]{1,0:T(4,128)} %refs_4_.1, ...), custom_call_target="tpu_custom_call" | custom-call | tf_op jit(solution)/shard_map/query/pallas_call | solution.py:664
  2.8 0.5 collective-permute-start.1
  3.4 2.6 %collective-permute-start.5 = (bf16[256,1024]{1,0:T(8,128)(2,1)}, bf16[256,1024]{1,0:T(8,128)(2,1)S(1)}, u32[]{:S(2)}, u32[]{:S(2)}) collective-permute-start(bf16[256,1024]{1,0:T(8,128)(2,1)} %refs_0_), channel_id=1, source_target_pairs={{0,2},{1,3},{2,0},{3,1},{4,6},{5,7},{6,4},{7,5},{8,10},{9,11},{10,... | collective-permute-start | bytes 1572872 | tf_op jit(solution)/shard_map/ppermute | solution.py:694
  5.9 1.5 %collective-permute-start = (bf16[80,128]{1,0:T(8,128)(2,1)}, bf16[80,128]{1,0:T(8,128)(2,1)S(1)}, u32[]{:S(2)}, u32[]{:S(2)}) collective-permute-start(bf16[80,128]{1,0:T(8,128)(2,1)} %get-tuple-element.42.refs_0_.query_far), channel_id=1, source_target_pairs={{0,4},{4,0},{8,12},{12,8},{16,20},{20,16},{24,28},{28,24},{1,5},{5... | collective-permute-start | bytes 61448 | tf_op jit(solution)/shard_map/ppermute | solution.py:698
  7.4 1.6 %copy-done.1 = bf16[32,128,2,128]{3,2,1,0:T(2,128)(2,1)S(1)} copy-done((bf16[32,128,2,128]{3,2,1,0:T(2,128)(2,1)S(1)}, bf16[32,128,2,128]{3,2,1,0:T(2,128)(2,1)}, u32[]{:S(2)}) %copy-start.1) | copy-done | bytes 2097176
  9.0 0.5 split_pages.1.cache
  9.9 3.6 %collective-permute-start.4 = (bf16[2,80,128]{2,1,0:T(8,128)(2,1)S(1)}, bf16[2,80,128]{2,1,0:T(8,128)(2,1)S(1)}, u32[]{:S(2)}, u32[]{:S(2)}) collective-permute-start(bf16[2,80,128]{2,1,0:T(8,128)(2,1)S(1)} %stack.1.refs_0_), channel_id=1, source_target_pairs={{0,24},{4,28},{8,16},{12,20},{16,8},{20,12},{24,0},{28,4},{1,25},{... | collective-permute-start | bytes 122888 | tf_op jit(solution)/shard_map/ppermute | solution.py:724
  13.6 0.8 %collective-permute-start.2 = (bf16[2,80,128]{2,1,0:T(8,128)(2,1)S(1)}, bf16[2,80,128]{2,1,0:T(8,128)(2,1)S(1)}, u32[]{:S(2)}, u32[]{:S(2)}) collective-permute-start(bf16[2,80,128]{2,1,0:T(8,128)(2,1)S(1)} %stack.1.refs_0_), channel_id=1, source_target_pairs={{0,8},{4,12},{8,0},{12,4},{16,24},{20,28},{24,16},{28,20},{1,9},{5... | collective-permute-start | bytes 122888 | tf_op jit(solution)/shard_map/ppermute | solution.py:724
  14.3 5.3 %tail.1 = bf16[4,24,128]{2,1,0:T(8,128)(2,1)} custom-call(s32[1,16]{1,0:T(1,128)} %lengths_far.3, bf16[80,128]{1,0:T(8,128)(2,1)} %get-tuple-element.42.refs_0_.query_far, bf16[32,1024]{1,0:T(8,128)(2,1)} %get-tuple-element.45.normed_far, f32[32,128]{1,0:T(8,128)} %get-tuple-element.46.cosine_far, f32[32,128]{1,0:T(8,128)} %get-tuple-element.47.sine_far, ...), custom_call_target="tpu_custom_call" | custom-call | flops 2000000000 | bytes 5000000 | tf_op jit(solution)/shard_map/tail/pallas_call | solution.py:731
  19.7 0.7 %copy-done.12 = bf16[4,24,128]{2,1,0:T(8,128)(2,1)S(1)} copy-done((bf16[4,24,128]{2,1,0:T(8,128)(2,1)S(1)}, bf16[4,24,128]{2,1,0:T(8,128)(2,1)}, u32[]{:S(2)}) %copy-start.12) | copy-done | bytes 24600
  20.4 2.9 %pages.2 = (bf16[32,24,128]{2,1,0:T(8,128)(2,1)}, bf16[8,16,128]{2,1,0:T(8,128)(2,1)S(1)}) custom-call(s32[256]{0:T(256)S(1)} %copy-done.10, s32[256]{0:T(256)S(1)} %copy-done.11, s32[8]{0:T(128)S(1)} %copy-done.9, bf16[32,256,128]{2,1,0:T(8,128)(2,1)S(1)} %split_pages.1.cache, bf16[4,24,128]{2,1,0:T(8,128)(2,1)S(1)} %copy-done.12, ...), custom_call_target="tpu_custom_call" | custom-call | flops 2000000000 | bytes 5000000 | tf_op jit(solution)/shard_map/pages/pallas_call | solution.py:754
  23.3 4.9 %all-to-all-start = ((bf16[32,24,128]{2,1,0:T(8,128)(2,1)}), bf16[32,24,128]{2,1,0:T(8,128)(2,1)S(1)}, u32[]{:S(2)}, u32[]{:S(2)}) async-start(bf16[32,24,128]{2,1,0:T(8,128)(2,1)} %get-tuple-element.51), calls=%async_computation | async-start | bytes 393216 | tf_op jit(solution)/shard_map/all_to_all | solution.py:771
  28.6 3.0 %prepare.1.refs_0_ = bf16[4,1024,256]{2,1,0:T(8,128)(2,1)} custom-call(bf16[4,2048,128]{2,1,0:T(8,128)(2,1)} %bitcast.37), custom_call_target="tpu_custom_call" | custom-call | flops 20000000000 | bytes 8000000 | tf_op jit(solution)/shard_map/prepare/pallas_call | solution.py:777
  32.1 5.0 %all-to-all-done = bf16[32,24,128]{2,1,0:T(8,128)(2,1)S(1)} async-done(((bf16[32,24,128]{2,1,0:T(8,128)(2,1)}), bf16[32,24,128]{2,1,0:T(8,128)(2,1)S(1)}, u32[]{:S(2)}, u32[]{:S(2)}) %all-to-all-start) | async-done | bytes 196640 | tf_op jit(solution)/shard_map/all_to_all | solution.py:771
  37.1 0.7 collective-permute-start.7
  37.8 1.0 %merge.1 = (bf16[16,16,512]{2,1,0:T(8,128)(2,1)S(1)}, f32[8,1024]{1,0:T(8,128)S(1)}) custom-call(bf16[8,4,24,128]{3,2,1,0:T(8,128)(2,1)S(1)} %bitcast.31, bf16[4,8,1024]{2,1,0:T(8,128)(2,1)S(1)} %copy-done.6, f32[3,1024]{1,0:T(4,128)S(1)} %copy-done.4, bf16[256,1024]{1,0:T(8,128)(2,1)S(1)} %copy-done.3, ...), custom_call_target="tpu_custom_call" | custom-call | tf_op jit(solution)/shard_map/merge/pallas_call | solution.py:813
  38.9 13.5 %all_to_all.15.arrived = bf16[16,16,512]{2,1,0:T(8,128)(2,1)S(1)} all-to-all(bf16[16,16,512]{2,1,0:T(8,128)(2,1)S(1)} %get-tuple-element.65), channel_id=1, replica_groups=mesh['req'=8,'tp_pair'=2,'tp_side'=2] {'req','tp_pair'}, dimensions={0} | all-to-all | bytes 524288 | tf_op jit(solution)/shard_map/all_to_all | solution.py:827
  52.4 1.4 %experts.1 = bf16[16,16,512]{2,1,0:T(8,128)(2,1)S(1)} custom-call(bf16[16,16,512]{2,1,0:T(8,128)(2,1)S(1)} %all_to_all.15.arrived, f32[128,32]{1,0:T(8,128)S(1)} %names.1.mask, bf16[32,1024]{1,0:T(8,128)(2,1)S(1)} %bitcast.32, bf16[4,1024,256]{2,1,0:T(8,128)(2,1)S(1)} %copy-done, bf16[4,1024,256]{2,1,0:T(8,128)(2,1)S(1)} %collective-permute-done.7.first_other, ...), custom_call_target="tpu_custom_call" | custom-call | tf_op jit(solution)/shard_map/experts/pallas_call | solution.py:838
  53.8 11.8 %all_to_all.16.arrived = bf16[8,2,16,512]{3,2,1,0:T(8,128)(2,1)S(1)} all-to-all(bf16[8,2,16,512]{3,2,1,0:T(8,128)(2,1)S(1)} %bitcast.30), channel_id=1, replica_groups=mesh['req'=8,'tp_pair'=2,'tp_side'=2] {'req'}, dimensions={0} | all-to-all | bytes 524288 | tf_op jit(solution)/shard_map/all_to_all | solution.py:847
  65.7 0.6 collective-permute-start.10
  66.4 1.2 %collective-permute-start.9 = (bf16[2,16,512]{2,1,0:T(8,128)(2,1)S(1)}, bf16[2,16,512]{2,1,0:T(8,128)(2,1)S(1)}, u32[]{:S(2)}, u32[]{:S(2)}) collective-permute-start(bf16[2,16,512]{2,1,0:T(8,128)(2,1)S(1)} %finish.1.refs_0_), channel_id=1, source_target_pairs={{0,1},{1,0},{2,3},{3,2},{4,5},{5,4},{6,7},{7,6},{8,9},{9,8},{10,11... | collective-permute-start | bytes 98312 | tf_op jit(solution)/shard_map/ppermute | solution.py:858
  67.6 1.5 %collective-permute-done.11.refs_3_ = bf16[2,16,512]{2,1,0:T(8,128)(2,1)S(1)} collective-permute-done((bf16[2,16,512]{2,1,0:T(8,128)(2,1)S(1)}, bf16[2,16,512]{2,1,0:T(8,128)(2,1)S(1)}, u32[]{:S(2)}, u32[]{:S(2)}) %collective-permute-start.11) | collective-permute-done | bytes 32800 | tf_op jit(solution)/shard_map/ppermute | solution.py:858
  69.0 0.7 collective-permute-done.10.refs_2_
  69.8 0.8 %score.1 = (bf16[256,128]{1,0:T(8,128)(2,1)}, f32[2,16]{1,0:T(2,128)}) custom-call(bf16[2,16,512]{2,1,0:T(8,128)(2,1)S(1)} %finish.1.refs_0_, bf16[2,16,512]{2,1,0:T(8,128)(2,1)S(1)} %collective-permute-done.9.refs_1_, bf16[2,16,512]{2,1,0:T(8,128)(2,1)S(1)} %collective-permute-done.10.refs_2_, bf16[2,16,512]{2,1,0:T(8,128)(2,1)S(1)} %collective-permute-done.11.refs_3_, ...), custom_call_target="tpu_custom_call" | custom-call | tf_op jit(solution)/shard_map/score/pallas_call | solution.py:861
  (42 shorter events, 1.5 us)
Async XLA Ops:
  2.8 16.8 %collective-permute-start.1 = (bf16[256,1024]{1,0:T(8,128)(2,1)}, bf16[256,1024]{1,0:T(8,128)(2,1)S(1)}, u32[]{:S(2)}, u32[]{:S(2)}) collective-permute-start(bf16[256,1024]{1,0:T(8,128)(2,1)} %refs_0_), channel_id=1, source_target_pairs={{0,1},{1,0},{2,3},{3,2},{4,5},{5,4},{6,7},{7,6},{8,9},{9,8},{10,11... | collective-permute-start | bytes 1572872 | tf_op jit(solution)/shard_map/ppermute | solution.py:695
  3.4 24.9 %collective-permute-start.5 = (bf16[256,1024]{1,0:T(8,128)(2,1)}, bf16[256,1024]{1,0:T(8,128)(2,1)S(1)}, u32[]{:S(2)}, u32[]{:S(2)}) collective-permute-start(bf16[256,1024]{1,0:T(8,128)(2,1)} %refs_0_), channel_id=1, source_target_pairs={{0,2},{1,3},{2,0},{3,1},{4,6},{5,7},{6,4},{7,5},{8,10},{9,11},{10,... | collective-permute-start | bytes 1572872 | tf_op jit(solution)/shard_map/ppermute | solution.py:694
  5.9 4.0 %collective-permute-start = (bf16[80,128]{1,0:T(8,128)(2,1)}, bf16[80,128]{1,0:T(8,128)(2,1)S(1)}, u32[]{:S(2)}, u32[]{:S(2)}) collective-permute-start(bf16[80,128]{1,0:T(8,128)(2,1)} %get-tuple-element.42.refs_0_.query_far), channel_id=1, source_target_pairs={{0,4},{4,0},{8,12},{12,8},{16,20},{20,16},{24,28},{28,24},{1,5},{5... | collective-permute-start | bytes 61448 | tf_op jit(solution)/shard_map/ppermute | solution.py:698
  7.4 1.6 %copy-start.1 = (bf16[32,128,2,128]{3,2,1,0:T(2,128)(2,1)S(1)}, bf16[32,128,2,128]{3,2,1,0:T(2,128)(2,1)}, u32[]{:S(2)}) copy-start(bf16[32,128,2,128]{3,2,1,0:T(2,128)(2,1)} %param.21) | copy-start | bytes 6291460
  9.9 9.7 %collective-permute-start.4 = (bf16[2,80,128]{2,1,0:T(8,128)(2,1)S(1)}, bf16[2,80,128]{2,1,0:T(8,128)(2,1)S(1)}, u32[]{:S(2)}, u32[]{:S(2)}) collective-permute-start(bf16[2,80,128]{2,1,0:T(8,128)(2,1)S(1)} %stack.1.refs_0_), channel_id=1, source_target_pairs={{0,24},{4,28},{8,16},{12,20},{16,8},{20,12},{24,0},{28,4},{1,25},{... | collective-permute-start | bytes 122888 | tf_op jit(solution)/shard_map/ppermute | solution.py:724
  13.5 6.1 %collective-permute-start.3 = (bf16[2,80,128]{2,1,0:T(8,128)(2,1)S(1)}, bf16[2,80,128]{2,1,0:T(8,128)(2,1)S(1)}, u32[]{:S(2)}, u32[]{:S(2)}) collective-permute-start(bf16[2,80,128]{2,1,0:T(8,128)(2,1)S(1)} %stack.1.refs_0_), channel_id=1, source_target_pairs={{0,16},{4,20},{8,24},{12,28},{16,0},{20,4},{24,8},{28,12},{1,17},{... | collective-permute-start | bytes 122888 | tf_op jit(solution)/shard_map/ppermute | solution.py:724
  13.6 6.1 %collective-permute-start.2 = (bf16[2,80,128]{2,1,0:T(8,128)(2,1)S(1)}, bf16[2,80,128]{2,1,0:T(8,128)(2,1)S(1)}, u32[]{:S(2)}, u32[]{:S(2)}) collective-permute-start(bf16[2,80,128]{2,1,0:T(8,128)(2,1)S(1)} %stack.1.refs_0_), channel_id=1, source_target_pairs={{0,8},{4,12},{8,0},{12,4},{16,24},{20,28},{24,16},{28,20},{1,9},{5... | collective-permute-start | bytes 122888 | tf_op jit(solution)/shard_map/ppermute | solution.py:724
  14.3 5.3 %copy-start.9 = (s32[8]{0:T(128)S(1)}, s32[8]{0:T(128)}, u32[]{:S(2)}) copy-start(s32[8]{0:T(128)} %lengths.1) | copy-start | bytes 100
  14.3 5.3 %copy-start.10 = (s32[256]{0:T(256)S(1)}, s32[256]{0:T(256)}, u32[]{:S(2)}) copy-start(s32[256]{0:T(256)} %homes.1) | copy-start | bytes 3076
  14.3 5.3 %copy-start.11 = (s32[256]{0:T(256)S(1)}, s32[256]{0:T(256)}, u32[]{:S(2)}) copy-start(s32[256]{0:T(256)} %pages.3) | copy-start | bytes 3076
  23.3 13.8 %all-to-all-start = ((bf16[32,24,128]{2,1,0:T(8,128)(2,1)}), bf16[32,24,128]{2,1,0:T(8,128)(2,1)S(1)}, u32[]{:S(2)}, u32[]{:S(2)}) async-start(bf16[32,24,128]{2,1,0:T(8,128)(2,1)} %get-tuple-element.51), calls=%async_computation | async-start | bytes 393216 | tf_op jit(solution)/shard_map/all_to_all | solution.py:771
  28.2 3.4 %collective-permute-start.6 = (bf16[256,1024]{1,0:T(8,128)(2,1)S(1)}, bf16[256,1024]{1,0:T(8,128)(2,1)S(1)}, u32[]{:S(2)}, u32[]{:S(2)}) collective-permute-start(bf16[256,1024]{1,0:T(8,128)(2,1)S(1)} %collective-permute-done.5.refs_2_), channel_id=1, source_target_pairs={{0,1},{1,0},{2,3},{3,2},{4,5},{5,4},{6,7},{7,6},{8,9},{9,8},{10,11... | collective-permute-start | bytes 1572872 | tf_op jit(solution)/shard_map/ppermute | solution.py:776
  32.1 5.7 %copy-start.3 = (bf16[256,1024]{1,0:T(8,128)(2,1)S(1)}, bf16[256,1024]{1,0:T(8,128)(2,1)}, u32[]{:S(2)}) copy-start(bf16[256,1024]{1,0:T(8,128)(2,1)} %refs_0_) | copy-start | bytes 1572868
  32.1 5.7 %copy-start.4 = (f32[3,1024]{1,0:T(4,128)S(1)}, f32[3,1024]{1,0:T(4,128)}, u32[]{:S(2)}) copy-start(f32[3,1024]{1,0:T(4,128)} %refs_4_.1) | copy-start | bytes 36868
  32.1 5.7 %copy-start.6 = (bf16[4,8,1024]{2,1,0:T(8,128)(2,1)S(1)}, bf16[4,8,1024]{2,1,0:T(8,128)(2,1)}, u32[]{:S(2)}) copy-start(bf16[4,8,1024]{2,1,0:T(8,128)(2,1)} %get-tuple-element.59.tokens) | copy-start | bytes 196612
  37.1 1.6 %copy-start.2 = (bf16[4,128,1024]{2,1,0:T(8,128)(2,1)S(1)}, bf16[4,128,1024]{2,1,0:T(8,128)(2,1)}, u32[]{:S(2)}) copy-start(bf16[4,128,1024]{2,1,0:T(8,128)(2,1)} %param.30) | copy-start | bytes 3145732
  37.1 15.3 %copy-start = (bf16[4,1024,256]{2,1,0:T(8,128)(2,1)S(1)}, bf16[4,1024,256]{2,1,0:T(8,128)(2,1)}, u32[]{:S(2)}) copy-start(bf16[4,1024,256]{2,1,0:T(8,128)(2,1)} %keep.1.first) | copy-start | bytes 6291460
  37.1 15.3 %copy-start.5 = (bf16[1024,32]{0,1:T(8,128)(2,1)S(1)}, bf16[1024,32]{0,1:T(8,128)(2,1)}, u32[]{:S(2)}) copy-start(bf16[1024,32]{0,1:T(8,128)(2,1)} %param.28) | copy-start | bytes 196612
  37.1 15.3 %collective-permute-start.7 = (bf16[4,1024,256]{2,1,0:T(8,128)(2,1)}, bf16[4,1024,256]{2,1,0:T(8,128)(2,1)S(1)}, u32[]{:S(2)}, u32[]{:S(2)}) collective-permute-start(bf16[4,1024,256]{2,1,0:T(8,128)(2,1)} %keep.1.first), channel_id=1, source_target_pairs={{0,1},{1,0},{2,3},{3,2},{4,5},{5,4},{6,7},{7,6},{8,9},{9,8},{10,11... | collective-permute-start | bytes 6291464 | tf_op jit(solution)/shard_map/ppermute | solution.py:811
  38.8 13.6 %collective-permute-start.8 = (bf16[512,1024]{1,0:T(8,128)(2,1)S(1)}, bf16[512,1024]{1,0:T(8,128)(2,1)S(1)}, u32[]{:S(2)}, u32[]{:S(2)}) collective-permute-start(bf16[512,1024]{1,0:T(8,128)(2,1)S(1)} %bitcast.28), channel_id=1, source_target_pairs={{0,1},{1,0},{2,3},{3,2},{4,5},{5,4},{6,7},{7,6},{8,9},{9,8},{10,11... | collective-permute-start | bytes 3145736 | tf_op jit(solution)/shard_map/ppermute | solution.py:826
  52.4 17.3 %copy-start.8 = (f32[1024]{0:T(1024)S(1)}, f32[1024]{0:T(1024)}, u32[]{:S(2)}) copy-start(f32[1024]{0:T(1024)} %param.31) | copy-start | bytes 12292
  65.6 3.4 %collective-permute-start.11 = (bf16[2,16,512]{2,1,0:T(8,128)(2,1)S(1)}, bf16[2,16,512]{2,1,0:T(8,128)(2,1)S(1)}, u32[]{:S(2)}, u32[]{:S(2)}) collective-permute-start(bf16[2,16,512]{2,1,0:T(8,128)(2,1)S(1)} %finish.1.refs_0_), channel_id=1, source_target_pairs={{0,3},{1,2},{2,1},{3,0},{4,7},{5,6},{6,5},{7,4},{8,11},{9,10},{10,... | collective-permute-start | bytes 98312 | tf_op jit(solution)/shard_map/ppermute | solution.py:858
  65.7 4.0 %collective-permute-start.10 = (bf16[2,16,512]{2,1,0:T(8,128)(2,1)S(1)}, bf16[2,16,512]{2,1,0:T(8,128)(2,1)S(1)}, u32[]{:S(2)}, u32[]{:S(2)}) collective-permute-start(bf16[2,16,512]{2,1,0:T(8,128)(2,1)S(1)} %finish.1.refs_0_), channel_id=1, source_target_pairs={{0,2},{1,3},{2,0},{3,1},{4,6},{5,7},{6,4},{7,5},{8,10},{9,11},{10,... | collective-permute-start | bytes 98312 | tf_op jit(solution)/shard_map/ppermute | solution.py:858
  66.4 3.4 %collective-permute-start.9 = (bf16[2,16,512]{2,1,0:T(8,128)(2,1)S(1)}, bf16[2,16,512]{2,1,0:T(8,128)(2,1)S(1)}, u32[]{:S(2)}, u32[]{:S(2)}) collective-permute-start(bf16[2,16,512]{2,1,0:T(8,128)(2,1)S(1)} %finish.1.refs_0_), channel_id=1, source_target_pairs={{0,1},{1,0},{2,3},{3,2},{4,5},{5,4},{6,7},{7,6},{8,9},{9,8},{10,11... | collective-permute-start | bytes 98312 | tf_op jit(solution)/shard_map/ppermute | solution.py:858
  (2 other events, 1.7 us)

commit v2 on v0

--- a/solution.py
+++ b/solution.py
@@ -266,11 +266,10 @@
     token_id = lane_iota(fresh.shape)
     fresh_seen = (token_id // fresh_count == row_sample) & (token_id % fresh_count <= row_fresh)
     fresh = jnp.where(fresh_seen, fresh, LOWEST)
-    for copy in blocks:
-        copy.wait()
     beside = []
     scores = []
     for part in range(parts):
+        blocks[part].wait()
         placed = [
             jnp.where(part_sample == a, wide[part], jnp.zeros_like(wide[part]))
             for a in range(per_part)
@@ -704,7 +703,7 @@
     across = [lax.ppermute(later, whole, flips[flip]) for flip in range(2, parts, 2)]
     beside = lax.ppermute(later, whole, flips[1])
     first_all = lax.all_to_all(message, "req", split_axis=0, concat_axis=0, tiled=True)
-    page_rows, tail, beside = lax.optimization_barrier((page_rows, tail, beside))
+    page_rows, tail = lax.optimization_barrier((page_rows, tail))
 
     step = 8 if pool % 8 == 0 else 1
     split_pages = pl.pallas_call(

time: 68.8 us -> 68.7 us (level)
  no operation moved by 1% of the time
where the time goes in v2:
time: 68.7 us; the launch traced here: 68.3 us
  blocking collectives  25.2 us (37%)
  Pallas kernels  17.7 us (26%)
  starting transfers between devices  15.6 us (23%)
  waiting for transfers between devices  8.81 us (13%)
  between operations  0.86 us (1%)
    all_to_all x1, blocking collectives, shards(): lax.all_to_all(message, ('req', 'tp_pair'), split_axis=0, concat_axis=0,...  13.5 us
    all_to_all x1, blocking collectives, shards(): lax.all_to_all(mixed, 'req', split_axis=0, concat_axis=0, tiled=True)  11.8 us
    all_to_all x1, starting transfers between devices, shards(): lax.all_to_all(message, 'req', split_axis=0, concat_axis=0, tiled=True)  5.81 us
    pallas_call x1, Pallas kernels, shards(): pl.pallas_call(functools.partial(tail_kernel, fresh_count), out_shape=jax...  5.33 us
    all_to_all x1, waiting for transfers between devices, shards(): lax.all_to_all(partial, ('req',) + whole, split_axis=0, concat_axis=0, ti...  5.03 us
    all_to_all x1, starting transfers between devices, shards(): lax.all_to_all(partial, ('req',) + whole, split_axis=0, concat_axis=0, ti...  3.74 us
    ppermute x1, starting transfers between devices, shards(): lax.ppermute(later, whole, flips[flip])  3.03 us
    pallas_call x1, Pallas kernels, shards(): pl.pallas_call(prepare_kernel, out_shape=jax.ShapeDtypeStruct((local, mod...  3.03 us
  transfers between devices with their start and end apart: 10, of which 4 were waited for; matrix products, arithmetic and copies ran while one was open for 0% of the time, Pallas kernels for 19%

profile of v2, /device:TPU:0, one launch (start us, length us, event | category | flops | bytes accessed | tf_op | source)
XLA Modules:
  0.0 68.3 jit_solution(10635141878582991124)
XLA Ops:
  0.6 2.3 %query.1 = (bf16[8,80,128]{2,1,0:T(8,128)(2,1)}, bf16[4,8,1024]{2,1,0:T(8,128)(2,1)}, bf16[32,1024]{1,0:T(8,128)(2,1)}, f32[32,128]{1,0:T(8,128)}, f32[32,128]{1,0:T(8,128)}) custom-call(s32[8]{0:T(128)} %lengths.1, s32[1,16]{1,0:T(1,128)} %lengths_far.3, bf16[256,128]{1,0:T(8,128)(2,1)} %bitcast.34, s32[16,16]{1,0:T(8,128)} %bitcast.35, f32[3,1024]{1,0:T(4,128)} %refs_4_.1, ...), custom_call_target="tpu_custom_call" | custom-call | tf_op jit(solution)/shard_map/query/pallas_call | solution.py:651
  2.9 3.0 %collective-permute-start = (bf16[256,1024]{1,0:T(8,128)(2,1)}, bf16[256,1024]{1,0:T(8,128)(2,1)S(1)}, u32[]{:S(2)}, u32[]{:S(2)}) collective-permute-start(bf16[256,1024]{1,0:T(8,128)(2,1)} %refs_0_), channel_id=1, source_target_pairs={{0,2},{1,3},{2,0},{3,1},{4,6},{5,7},{6,4},{7,5},{8,10},{9,11},{10,... | collective-permute-start | bytes 1572872 | tf_op jit(solution)/shard_map/ppermute | solution.py:703
  5.9 5.8 %all-to-all-start = ((bf16[8,80,128]{2,1,0:T(8,128)(2,1)}), bf16[8,80,128]{2,1,0:T(8,128)(2,1)S(1)}, u32[]{:S(2)}, u32[]{:S(2)}) async-start(bf16[8,80,128]{2,1,0:T(8,128)(2,1)} %get-tuple-element.36.query_far), calls=%async_computation | async-start | bytes 327680 | tf_op jit(solution)/shard_map/all_to_all | solution.py:705
  11.8 5.3 %tail.1 = bf16[4,24,128]{2,1,0:T(8,128)(2,1)} custom-call(s32[1,16]{1,0:T(1,128)} %lengths_far.3, bf16[8,80,128]{2,1,0:T(8,128)(2,1)} %get-tuple-element.36.query_far, bf16[32,1024]{1,0:T(8,128)(2,1)} %get-tuple-element.31.normed_far, f32[32,128]{1,0:T(8,128)} %get-tuple-element.32.cosine_far, f32[32,128]{1,0:T(8,128)} %get-tuple-element.33.sine_far, ...), custom_call_target="tpu_custom_call" | custom-call | flops 2000000000 | bytes 5000000 | tf_op jit(solution)/shard_map/tail/pallas_call | solution.py:680
  17.2 0.6 split_pages.1.cache
  17.7 1.6 %all-to-all-done.query = bf16[8,80,128]{2,1,0:T(8,128)(2,1)S(1)} async-done(((bf16[8,80,128]{2,1,0:T(8,128)(2,1)}), bf16[8,80,128]{2,1,0:T(8,128)(2,1)S(1)}, u32[]{:S(2)}, u32[]{:S(2)}) %all-to-all-start) | async-done | bytes 163872 | tf_op jit(solution)/shard_map/all_to_all | solution.py:705
  19.3 2.9 %pages.2 = (bf16[32,24,128]{2,1,0:T(8,128)(2,1)}, bf16[8,16,128]{2,1,0:T(8,128)(2,1)S(1)}) custom-call(s32[256]{0:T(256)S(1)} %copy-done.9, s32[256]{0:T(256)S(1)} %copy-done.10, s32[8]{0:T(128)S(1)} %copy-done.8, bf16[32,256,128]{2,1,0:T(8,128)(2,1)S(1)} %split_pages.1.cache, bf16[4,24,128]{2,1,0:T(8,128)(2,1)S(1)} %copy-done.11, ...), custom_call_target="tpu_custom_call" | custom-call | flops 2000000000 | bytes 5000000 | tf_op jit(solution)/shard_map/pages/pallas_call | solution.py:721
  22.2 3.7 %all-to-all-start.1 = ((bf16[32,24,128]{2,1,0:T(8,128)(2,1)}), bf16[32,24,128]{2,1,0:T(8,128)(2,1)S(1)}, u32[]{:S(2)}, u32[]{:S(2)}) async-start(bf16[32,24,128]{2,1,0:T(8,128)(2,1)} %get-tuple-element.37), calls=%async_computation.1 | async-start | bytes 393216 | tf_op jit(solution)/shard_map/all_to_all | solution.py:737
  26.0 0.3 collective-permute-start.2
  26.3 3.0 %prepare.1.refs_0_ = bf16[4,1024,256]{2,1,0:T(8,128)(2,1)} custom-call(bf16[4,2048,128]{2,1,0:T(8,128)(2,1)} %bitcast.37), custom_call_target="tpu_custom_call" | custom-call | flops 20000000000 | bytes 8000000 | tf_op jit(solution)/shard_map/prepare/pallas_call | solution.py:743
  29.4 0.4 names.1.mask
  29.8 5.0 %all-to-all-done.1 = bf16[32,24,128]{2,1,0:T(8,128)(2,1)S(1)} async-done(((bf16[32,24,128]{2,1,0:T(8,128)(2,1)}), bf16[32,24,128]{2,1,0:T(8,128)(2,1)S(1)}, u32[]{:S(2)}, u32[]{:S(2)}) %all-to-all-start.1) | async-done | bytes 196640 | tf_op jit(solution)/shard_map/all_to_all | solution.py:737
  34.9 0.7 collective-permute-start.3
  35.5 1.0 %merge.1 = (bf16[16,16,512]{2,1,0:T(8,128)(2,1)S(1)}, f32[8,1024]{1,0:T(8,128)S(1)}) custom-call(bf16[8,4,24,128]{3,2,1,0:T(8,128)(2,1)S(1)} %bitcast.31, bf16[4,8,1024]{2,1,0:T(8,128)(2,1)S(1)} %copy-done.6, f32[3,1024]{1,0:T(4,128)S(1)} %copy-done.4, bf16[256,1024]{1,0:T(8,128)(2,1)S(1)} %copy-done.3, ...), custom_call_target="tpu_custom_call" | custom-call | tf_op jit(solution)/shard_map/merge/pallas_call | solution.py:779
  36.5 0.2 collective-permute-start.4
  36.7 13.5 %all_to_all.20.arrived = bf16[16,16,512]{2,1,0:T(8,128)(2,1)S(1)} all-to-all(bf16[16,16,512]{2,1,0:T(8,128)(2,1)S(1)} %get-tuple-element.51), channel_id=1, replica_groups=mesh['req'=8,'tp_pair'=2,'tp_side'=2] {'req','tp_pair'}, dimensions={0} | all-to-all | bytes 524288 | tf_op jit(solution)/shard_map/all_to_all | solution.py:793
  50.2 1.4 %experts.1 = bf16[16,16,512]{2,1,0:T(8,128)(2,1)S(1)} custom-call(bf16[16,16,512]{2,1,0:T(8,128)(2,1)S(1)} %all_to_all.20.arrived, f32[128,32]{1,0:T(8,128)S(1)} %names.1.mask, bf16[32,1024]{1,0:T(8,128)(2,1)S(1)} %bitcast.32, bf16[4,1024,256]{2,1,0:T(8,128)(2,1)S(1)} %copy-done, bf16[4,1024,256]{2,1,0:T(8,128)(2,1)S(1)} %collective-permute-done.3.first_other, ...), custom_call_target="tpu_custom_call" | custom-call | tf_op jit(solution)/shard_map/experts/pallas_call | solution.py:804
  51.6 11.8 %all_to_all.21.arrived = bf16[8,2,16,512]{3,2,1,0:T(8,128)(2,1)S(1)} all-to-all(bf16[8,2,16,512]{3,2,1,0:T(8,128)(2,1)S(1)} %bitcast.30), channel_id=1, replica_groups=mesh['req'=8,'tp_pair'=2,'tp_side'=2] {'req'}, dimensions={0} | all-to-all | bytes 524288 | tf_op jit(solution)/shard_map/all_to_all | solution.py:813
  63.4 0.1 collective-permute-start.7
  63.5 0.6 collective-permute-start.6
  64.1 1.2 %collective-permute-start.5 = (bf16[2,16,512]{2,1,0:T(8,128)(2,1)S(1)}, bf16[2,16,512]{2,1,0:T(8,128)(2,1)S(1)}, u32[]{:S(2)}, u32[]{:S(2)}) collective-permute-start(bf16[2,16,512]{2,1,0:T(8,128)(2,1)S(1)} %finish.1.refs_0_), channel_id=1, source_target_pairs={{0,1},{1,0},{2,3},{3,2},{4,5},{5,4},{6,7},{7,6},{8,9},{9,8},{10,11... | collective-permute-start | bytes 98312 | tf_op jit(solution)/shard_map/ppermute | solution.py:824
  65.3 1.5 %collective-permute-done.7.refs_3_ = bf16[2,16,512]{2,1,0:T(8,128)(2,1)S(1)} collective-permute-done((bf16[2,16,512]{2,1,0:T(8,128)(2,1)S(1)}, bf16[2,16,512]{2,1,0:T(8,128)(2,1)S(1)}, u32[]{:S(2)}, u32[]{:S(2)}) %collective-permute-start.7) | collective-permute-done | bytes 32800 | tf_op jit(solution)/shard_map/ppermute | solution.py:824
  66.8 0.7 %collective-permute-done.6.refs_2_ = bf16[2,16,512]{2,1,0:T(8,128)(2,1)S(1)} collective-permute-done((bf16[2,16,512]{2,1,0:T(8,128)(2,1)S(1)}, bf16[2,16,512]{2,1,0:T(8,128)(2,1)S(1)}, u32[]{:S(2)}, u32[]{:S(2)}) %collective-permute-start.6) | collective-permute-done | bytes 32800 | tf_op jit(solution)/shard_map/ppermute | solution.py:824
  67.5 0.8 %score.1 = (bf16[256,128]{1,0:T(8,128)(2,1)}, f32[2,16]{1,0:T(2,128)}) custom-call(bf16[2,16,512]{2,1,0:T(8,128)(2,1)S(1)} %finish.1.refs_0_, bf16[2,16,512]{2,1,0:T(8,128)(2,1)S(1)} %collective-permute-done.5.refs_1_, bf16[2,16,512]{2,1,0:T(8,128)(2,1)S(1)} %collective-permute-done.6.refs_2_, bf16[2,16,512]{2,1,0:T(8,128)(2,1)S(1)} %collective-permute-done.7.refs_3_, ...), custom_call_target="tpu_custom_call" | custom-call | tf_op jit(solution)/shard_map/score/pallas_call | solution.py:827
  (33 shorter events, 0.1 us)
Async XLA Ops:
  2.9 23.1 %collective-permute-start = (bf16[256,1024]{1,0:T(8,128)(2,1)}, bf16[256,1024]{1,0:T(8,128)(2,1)S(1)}, u32[]{:S(2)}, u32[]{:S(2)}) collective-permute-start(bf16[256,1024]{1,0:T(8,128)(2,1)} %refs_0_), channel_id=1, source_target_pairs={{0,2},{1,3},{2,0},{3,1},{4,6},{5,7},{6,4},{7,5},{8,10},{9,11},{10,... | collective-permute-start | bytes 1572872 | tf_op jit(solution)/shard_map/ppermute | solution.py:703
  5.9 13.4 %all-to-all-start = ((bf16[8,80,128]{2,1,0:T(8,128)(2,1)}), bf16[8,80,128]{2,1,0:T(8,128)(2,1)S(1)}, u32[]{:S(2)}, u32[]{:S(2)}) async-start(bf16[8,80,128]{2,1,0:T(8,128)(2,1)} %get-tuple-element.36.query_far), calls=%async_computation | async-start | bytes 327680 | tf_op jit(solution)/shard_map/all_to_all | solution.py:705
  11.7 17.6 %collective-permute-start.1 = (bf16[256,1024]{1,0:T(8,128)(2,1)}, bf16[256,1024]{1,0:T(8,128)(2,1)S(1)}, u32[]{:S(2)}, u32[]{:S(2)}) collective-permute-start(bf16[256,1024]{1,0:T(8,128)(2,1)} %refs_0_), channel_id=1, source_target_pairs={{0,1},{1,0},{2,3},{3,2},{4,5},{5,4},{6,7},{7,6},{8,9},{9,8},{10,11... | collective-permute-start | bytes 1572872 | tf_op jit(solution)/shard_map/ppermute | solution.py:704
  11.7 5.3 %copy-start.1 = (bf16[32,128,2,128]{3,2,1,0:T(2,128)(2,1)S(1)}, bf16[32,128,2,128]{3,2,1,0:T(2,128)(2,1)}, u32[]{:S(2)}) copy-start(bf16[32,128,2,128]{3,2,1,0:T(2,128)(2,1)} %param.21) | copy-start | bytes 6291460
  17.1 2.2 %copy-start.8 = (s32[8]{0:T(128)S(1)}, s32[8]{0:T(128)}, u32[]{:S(2)}) copy-start(s32[8]{0:T(128)} %lengths.1) | copy-start | bytes 100
  17.1 2.2 %copy-start.9 = (s32[256]{0:T(256)S(1)}, s32[256]{0:T(256)}, u32[]{:S(2)}) copy-start(s32[256]{0:T(256)} %homes.1) | copy-start | bytes 3076
  17.1 2.2 %copy-start.10 = (s32[256]{0:T(256)S(1)}, s32[256]{0:T(256)}, u32[]{:S(2)}) copy-start(s32[256]{0:T(256)} %pages.3) | copy-start | bytes 3076
  17.1 2.2 %copy-start.11 = (bf16[4,24,128]{2,1,0:T(8,128)(2,1)S(1)}, bf16[4,24,128]{2,1,0:T(8,128)(2,1)}, u32[]{:S(2)}) copy-start(bf16[4,24,128]{2,1,0:T(8,128)(2,1)} %tail.1) | copy-start | bytes 73732
  22.2 12.6 %all-to-all-start.1 = ((bf16[32,24,128]{2,1,0:T(8,128)(2,1)}), bf16[32,24,128]{2,1,0:T(8,128)(2,1)S(1)}, u32[]{:S(2)}, u32[]{:S(2)}) async-start(bf16[32,24,128]{2,1,0:T(8,128)(2,1)} %get-tuple-element.37), calls=%async_computation.1 | async-start | bytes 393216 | tf_op jit(solution)/shard_map/all_to_all | solution.py:737
  26.0 3.4 %collective-permute-start.2 = (bf16[256,1024]{1,0:T(8,128)(2,1)S(1)}, bf16[256,1024]{1,0:T(8,128)(2,1)S(1)}, u32[]{:S(2)}, u32[]{:S(2)}) collective-permute-start(bf16[256,1024]{1,0:T(8,128)(2,1)S(1)} %collective-permute-done.refs_2_), channel_id=1, source_target_pairs={{0,1},{1,0},{2,3},{3,2},{4,5},{5,4},{6,7},{7,6},{8,9},{9,8},{10,11... | collective-permute-start | bytes 1572872 | tf_op jit(solution)/shard_map/ppermute | solution.py:742
  29.8 5.7 %copy-start.3 = (bf16[256,1024]{1,0:T(8,128)(2,1)S(1)}, bf16[256,1024]{1,0:T(8,128)(2,1)}, u32[]{:S(2)}) copy-start(bf16[256,1024]{1,0:T(8,128)(2,1)} %refs_0_) | copy-start | bytes 1572868
  29.8 5.7 %copy-start.4 = (f32[3,1024]{1,0:T(4,128)S(1)}, f32[3,1024]{1,0:T(4,128)}, u32[]{:S(2)}) copy-start(f32[3,1024]{1,0:T(4,128)} %refs_4_.1) | copy-start | bytes 36868
  29.8 5.7 %copy-start.6 = (bf16[4,8,1024]{2,1,0:T(8,128)(2,1)S(1)}, bf16[4,8,1024]{2,1,0:T(8,128)(2,1)}, u32[]{:S(2)}) copy-start(bf16[4,8,1024]{2,1,0:T(8,128)(2,1)} %get-tuple-element.45.tokens) | copy-start | bytes 196612
  34.9 1.6 %copy-start.2 = (bf16[4,128,1024]{2,1,0:T(8,128)(2,1)S(1)}, bf16[4,128,1024]{2,1,0:T(8,128)(2,1)}, u32[]{:S(2)}) copy-start(bf16[4,128,1024]{2,1,0:T(8,128)(2,1)} %param.30) | copy-start | bytes 3145732
  34.9 15.3 %copy-start = (bf16[4,1024,256]{2,1,0:T(8,128)(2,1)S(1)}, bf16[4,1024,256]{2,1,0:T(8,128)(2,1)}, u32[]{:S(2)}) copy-start(bf16[4,1024,256]{2,1,0:T(8,128)(2,1)} %keep.1.first) | copy-start | bytes 6291460
  34.9 15.3 %copy-start.5 = (bf16[1024,32]{0,1:T(8,128)(2,1)S(1)}, bf16[1024,32]{0,1:T(8,128)(2,1)}, u32[]{:S(2)}) copy-start(bf16[1024,32]{0,1:T(8,128)(2,1)} %param.28) | copy-start | bytes 196612
  34.9 15.3 %collective-permute-start.3 = (bf16[4,1024,256]{2,1,0:T(8,128)(2,1)}, bf16[4,1024,256]{2,1,0:T(8,128)(2,1)S(1)}, u32[]{:S(2)}, u32[]{:S(2)}) collective-permute-start(bf16[4,1024,256]{2,1,0:T(8,128)(2,1)} %keep.1.first), channel_id=1, source_target_pairs={{0,1},{1,0},{2,3},{3,2},{4,5},{5,4},{6,7},{7,6},{8,9},{9,8},{10,11... | collective-permute-start | bytes 6291464 | tf_op jit(solution)/shard_map/ppermute | solution.py:777
  36.5 13.6 %collective-permute-start.4 = (bf16[512,1024]{1,0:T(8,128)(2,1)S(1)}, bf16[512,1024]{1,0:T(8,128)(2,1)S(1)}, u32[]{:S(2)}, u32[]{:S(2)}) collective-permute-start(bf16[512,1024]{1,0:T(8,128)(2,1)S(1)} %bitcast.28), channel_id=1, source_target_pairs={{0,1},{1,0},{2,3},{3,2},{4,5},{5,4},{6,7},{7,6},{8,9},{9,8},{10,11... | collective-permute-start | bytes 3145736 | tf_op jit(solution)/shard_map/ppermute | solution.py:792
  50.2 17.3 %copy-start.7 = (f32[1024]{0:T(1024)S(1)}, f32[1024]{0:T(1024)}, u32[]{:S(2)}) copy-start(f32[1024]{0:T(1024)} %param.31) | copy-start | bytes 12292
  63.4 3.4 %collective-permute-start.7 = (bf16[2,16,512]{2,1,0:T(8,128)(2,1)S(1)}, bf16[2,16,512]{2,1,0:T(8,128)(2,1)S(1)}, u32[]{:S(2)}, u32[]{:S(2)}) collective-permute-start(bf16[2,16,512]{2,1,0:T(8,128)(2,1)S(1)} %finish.1.refs_0_), channel_id=1, source_target_pairs={{0,3},{1,2},{2,1},{3,0},{4,7},{5,6},{6,5},{7,4},{8,11},{9,10},{10,... | collective-permute-start | bytes 98312 | tf_op jit(solution)/shard_map/ppermute | solution.py:824
  63.5 4.0 %collective-permute-start.6 = (bf16[2,16,512]{2,1,0:T(8,128)(2,1)S(1)}, bf16[2,16,512]{2,1,0:T(8,128)(2,1)S(1)}, u32[]{:S(2)}, u32[]{:S(2)}) collective-permute-start(bf16[2,16,512]{2,1,0:T(8,128)(2,1)S(1)} %finish.1.refs_0_), channel_id=1, source_target_pairs={{0,2},{1,3},{2,0},{3,1},{4,6},{5,7},{6,4},{7,5},{8,10},{9,11},{10,... | collective-permute-start | bytes 98312 | tf_op jit(solution)/shard_map/ppermute | solution.py:824
  64.1 3.4 %collective-permute-start.5 = (bf16[2,16,512]{2,1,0:T(8,128)(2,1)S(1)}, bf16[2,16,512]{2,1,0:T(8,128)(2,1)S(1)}, u32[]{:S(2)}, u32[]{:S(2)}) collective-permute-start(bf16[2,16,512]{2,1,0:T(8,128)(2,1)S(1)} %finish.1.refs_0_), channel_id=1, source_target_pairs={{0,1},{1,0},{2,3},{3,2},{4,5},{5,4},{6,7},{7,6},{8,9},{9,8},{10,11... | collective-permute-start | bytes 98312 | tf_op jit(solution)/shard_map/ppermute | solution.py:824

commit v3 on v2

--- a/solution.py
+++ b/solution.py
@@ -694,7 +694,7 @@
             pltpu.SemaphoreType.DMA((parts,)),
         ],
         compiler_params=params(HOLD_MIB),
-        cost_estimate=cost(2e9, 5e6),
+        cost_estimate=cost(2e10, 5e6),
         name="tail",
     )(tail_len, *tail_inputs, key_value_rows, tail_rows)
 

time: 68.7 us -> 68.7 us (level)
  no operation moved by 1% of the time
where the time goes in v3:
time: 68.7 us; the launch traced here: 68.3 us
  blocking collectives  25.2 us (37%)
  Pallas kernels  17.7 us (26%)
  starting transfers between devices  15.4 us (22%)
  waiting for transfers between devices  9.07 us (13%)
  between operations  0.85 us (1%)
    all_to_all x1, blocking collectives, shards(): lax.all_to_all(message, ('req', 'tp_pair'), split_axis=0, concat_axis=0,...  13.5 us
    all_to_all x1, blocking collectives, shards(): lax.all_to_all(mixed, 'req', split_axis=0, concat_axis=0, tiled=True)  11.8 us
    all_to_all x1, starting transfers between devices, shards(): lax.all_to_all(message, 'req', split_axis=0, concat_axis=0, tiled=True)  5.81 us
    pallas_call x1, Pallas kernels, shards(): pl.pallas_call(functools.partial(tail_kernel, fresh_count), out_shape=jax...  5.32 us
    all_to_all x1, waiting for transfers between devices, shards(): lax.all_to_all(partial, ('req',) + whole, split_axis=0, concat_axis=0, ti...  5.03 us
    all_to_all x1, starting transfers between devices, shards(): lax.all_to_all(partial, ('req',) + whole, split_axis=0, concat_axis=0, ti...  3.4 us
    pallas_call x1, Pallas kernels, shards(): pl.pallas_call(prepare_kernel, out_shape=jax.ShapeDtypeStruct((local, mod...  3.03 us
    pallas_call x1, Pallas kernels, shards(): pl.pallas_call(functools.partial(page_kernel, slot_cap), out_shape=(jax.S...  2.9 us
  transfers between devices with their start and end apart: 10, of which 4 were waited for; matrix products, arithmetic and copies ran while one was open for 0% of the time, Pallas kernels for 19%

profile of v3, /device:TPU:0, one launch (start us, length us, event | category | flops | bytes accessed | tf_op | source)
XLA Modules:
  0.0 68.3 jit_solution(10311175842897098593)
XLA Ops:
  0.6 2.3 %query.1 = (bf16[8,80,128]{2,1,0:T(8,128)(2,1)}, bf16[4,8,1024]{2,1,0:T(8,128)(2,1)}, bf16[32,1024]{1,0:T(8,128)(2,1)}, f32[32,128]{1,0:T(8,128)}, f32[32,128]{1,0:T(8,128)}) custom-call(s32[8]{0:T(128)} %lengths.1, s32[1,16]{1,0:T(1,128)} %lengths_far.3, bf16[256,128]{1,0:T(8,128)(2,1)} %bitcast.34, s32[16,16]{1,0:T(8,128)} %bitcast.35, f32[3,1024]{1,0:T(4,128)} %refs_4_.1, ...), custom_call_target="tpu_custom_call" | custom-call | tf_op jit(solution)/shard_map/query/pallas_call | solution.py:651
  2.9 0.5 collective-permute-start.1
  3.4 2.6 %collective-permute-start = (bf16[256,1024]{1,0:T(8,128)(2,1)}, bf16[256,1024]{1,0:T(8,128)(2,1)S(1)}, u32[]{:S(2)}, u32[]{:S(2)}) collective-permute-start(bf16[256,1024]{1,0:T(8,128)(2,1)} %refs_0_), channel_id=1, source_target_pairs={{0,2},{1,3},{2,0},{3,1},{4,6},{5,7},{6,4},{7,5},{8,10},{9,11},{10,... | collective-permute-start | bytes 1572872 | tf_op jit(solution)/shard_map/ppermute | solution.py:703
  6.0 5.8 %all-to-all-start = ((bf16[8,80,128]{2,1,0:T(8,128)(2,1)}), bf16[8,80,128]{2,1,0:T(8,128)(2,1)S(1)}, u32[]{:S(2)}, u32[]{:S(2)}) async-start(bf16[8,80,128]{2,1,0:T(8,128)(2,1)} %get-tuple-element.36.query_far), calls=%async_computation | async-start | bytes 327680 | tf_op jit(solution)/shard_map/all_to_all | solution.py:705
  11.8 5.3 %tail.1 = bf16[4,24,128]{2,1,0:T(8,128)(2,1)} custom-call(s32[1,16]{1,0:T(1,128)} %lengths_far.3, bf16[8,80,128]{2,1,0:T(8,128)(2,1)} %get-tuple-element.36.query_far, bf16[32,1024]{1,0:T(8,128)(2,1)} %get-tuple-element.31.normed_far, f32[32,128]{1,0:T(8,128)} %get-tuple-element.32.cosine_far, f32[32,128]{1,0:T(8,128)} %get-tuple-element.33.sine_far, ...), custom_call_target="tpu_custom_call" | custom-call | flops 20000000000 | bytes 5000000 | tf_op jit(solution)/shard_map/tail/pallas_call | solution.py:680
  17.2 0.6 split_pages.1.cache
  17.8 1.8 %all-to-all-done.query = bf16[8,80,128]{2,1,0:T(8,128)(2,1)S(1)} async-done(((bf16[8,80,128]{2,1,0:T(8,128)(2,1)}), bf16[8,80,128]{2,1,0:T(8,128)(2,1)S(1)}, u32[]{:S(2)}, u32[]{:S(2)}) %all-to-all-start) | async-done | bytes 163872 | tf_op jit(solution)/shard_map/all_to_all | solution.py:705
  19.6 2.9 %pages.2 = (bf16[32,24,128]{2,1,0:T(8,128)(2,1)}, bf16[8,16,128]{2,1,0:T(8,128)(2,1)S(1)}) custom-call(s32[256]{0:T(256)S(1)} %copy-done.9, s32[256]{0:T(256)S(1)} %copy-done.10, s32[8]{0:T(128)S(1)} %copy-done.8, bf16[32,256,128]{2,1,0:T(8,128)(2,1)S(1)} %split_pages.1.cache, bf16[4,24,128]{2,1,0:T(8,128)(2,1)S(1)} %copy-done.11, ...), custom_call_target="tpu_custom_call" | custom-call | flops 2000000000 | bytes 5000000 | tf_op jit(solution)/shard_map/pages/pallas_call | solution.py:721
  22.5 3.4 %all-to-all-start.1 = ((bf16[32,24,128]{2,1,0:T(8,128)(2,1)}), bf16[32,24,128]{2,1,0:T(8,128)(2,1)S(1)}, u32[]{:S(2)}, u32[]{:S(2)}) async-start(bf16[32,24,128]{2,1,0:T(8,128)(2,1)} %get-tuple-element.37), calls=%async_computation.1 | async-start | bytes 393216 | tf_op jit(solution)/shard_map/all_to_all | solution.py:737
  26.0 0.3 collective-permute-start.2
  26.3 3.0 %prepare.1.refs_0_ = bf16[4,1024,256]{2,1,0:T(8,128)(2,1)} custom-call(bf16[4,2048,128]{2,1,0:T(8,128)(2,1)} %bitcast.37), custom_call_target="tpu_custom_call" | custom-call | flops 20000000000 | bytes 8000000 | tf_op jit(solution)/shard_map/prepare/pallas_call | solution.py:743
  29.3 0.4 names.1.mask
  29.8 5.0 %all-to-all-done.1 = bf16[32,24,128]{2,1,0:T(8,128)(2,1)S(1)} async-done(((bf16[32,24,128]{2,1,0:T(8,128)(2,1)}), bf16[32,24,128]{2,1,0:T(8,128)(2,1)S(1)}, u32[]{:S(2)}, u32[]{:S(2)}) %all-to-all-start.1) | async-done | bytes 196640 | tf_op jit(solution)/shard_map/all_to_all | solution.py:737
  34.8 0.7 collective-permute-start.3
  35.5 1.0 %merge.1 = (bf16[16,16,512]{2,1,0:T(8,128)(2,1)S(1)}, f32[8,1024]{1,0:T(8,128)S(1)}) custom-call(bf16[8,4,24,128]{3,2,1,0:T(8,128)(2,1)S(1)} %bitcast.31, bf16[4,8,1024]{2,1,0:T(8,128)(2,1)S(1)} %copy-done.6, f32[3,1024]{1,0:T(4,128)S(1)} %copy-done.4, bf16[256,1024]{1,0:T(8,128)(2,1)S(1)} %copy-done.3, ...), custom_call_target="tpu_custom_call" | custom-call | tf_op jit(solution)/shard_map/merge/pallas_call | solution.py:779
  36.5 0.2 collective-permute-start.4
  36.6 13.5 %all_to_all.20.arrived = bf16[16,16,512]{2,1,0:T(8,128)(2,1)S(1)} all-to-all(bf16[16,16,512]{2,1,0:T(8,128)(2,1)S(1)} %get-tuple-element.51), channel_id=1, replica_groups=mesh['req'=8,'tp_pair'=2,'tp_side'=2] {'req','tp_pair'}, dimensions={0} | all-to-all | bytes 524288 | tf_op jit(solution)/shard_map/all_to_all | solution.py:793
  50.2 1.4 %experts.1 = bf16[16,16,512]{2,1,0:T(8,128)(2,1)S(1)} custom-call(bf16[16,16,512]{2,1,0:T(8,128)(2,1)S(1)} %all_to_all.20.arrived, f32[128,32]{1,0:T(8,128)S(1)} %names.1.mask, bf16[32,1024]{1,0:T(8,128)(2,1)S(1)} %bitcast.32, bf16[4,1024,256]{2,1,0:T(8,128)(2,1)S(1)} %copy-done, bf16[4,1024,256]{2,1,0:T(8,128)(2,1)S(1)} %collective-permute-done.3.first_other, ...), custom_call_target="tpu_custom_call" | custom-call | tf_op jit(solution)/shard_map/experts/pallas_call | solution.py:804
  51.5 11.8 %all_to_all.21.arrived = bf16[8,2,16,512]{3,2,1,0:T(8,128)(2,1)S(1)} all-to-all(bf16[8,2,16,512]{3,2,1,0:T(8,128)(2,1)S(1)} %bitcast.30), channel_id=1, replica_groups=mesh['req'=8,'tp_pair'=2,'tp_side'=2] {'req'}, dimensions={0} | all-to-all | bytes 524288 | tf_op jit(solution)/shard_map/all_to_all | solution.py:813
  63.4 0.6 collective-permute-start.6
  64.1 1.2 %collective-permute-start.5 = (bf16[2,16,512]{2,1,0:T(8,128)(2,1)S(1)}, bf16[2,16,512]{2,1,0:T(8,128)(2,1)S(1)}, u32[]{:S(2)}, u32[]{:S(2)}) collective-permute-start(bf16[2,16,512]{2,1,0:T(8,128)(2,1)S(1)} %finish.1.refs_0_), channel_id=1, source_target_pairs={{0,1},{1,0},{2,3},{3,2},{4,5},{5,4},{6,7},{7,6},{8,9},{9,8},{10,11... | collective-permute-start | bytes 98312 | tf_op jit(solution)/shard_map/ppermute | solution.py:824
  65.3 1.5 %collective-permute-done.7.refs_3_ = bf16[2,16,512]{2,1,0:T(8,128)(2,1)S(1)} collective-permute-done((bf16[2,16,512]{2,1,0:T(8,128)(2,1)S(1)}, bf16[2,16,512]{2,1,0:T(8,128)(2,1)S(1)}, u32[]{:S(2)}, u32[]{:S(2)}) %collective-permute-start.7) | collective-permute-done | bytes 32800 | tf_op jit(solution)/shard_map/ppermute | solution.py:824
  66.8 0.7 %collective-permute-done.6.refs_2_ = bf16[2,16,512]{2,1,0:T(8,128)(2,1)S(1)} collective-permute-done((bf16[2,16,512]{2,1,0:T(8,128)(2,1)S(1)}, bf16[2,16,512]{2,1,0:T(8,128)(2,1)S(1)}, u32[]{:S(2)}, u32[]{:S(2)}) %collective-permute-start.6) | collective-permute-done | bytes 32800 | tf_op jit(solution)/shard_map/ppermute | solution.py:824
  67.5 0.8 %score.1 = (bf16[256,128]{1,0:T(8,128)(2,1)}, f32[2,16]{1,0:T(2,128)}) custom-call(bf16[2,16,512]{2,1,0:T(8,128)(2,1)S(1)} %finish.1.refs_0_, bf16[2,16,512]{2,1,0:T(8,128)(2,1)S(1)} %collective-permute-done.5.refs_1_, bf16[2,16,512]{2,1,0:T(8,128)(2,1)S(1)} %collective-permute-done.6.refs_2_, bf16[2,16,512]{2,1,0:T(8,128)(2,1)S(1)} %collective-permute-done.7.refs_3_, ...), custom_call_target="tpu_custom_call" | custom-call | tf_op jit(solution)/shard_map/score/pallas_call | solution.py:827
  (33 shorter events, 0.2 us)
Async XLA Ops:
  2.9 26.4 %collective-permute-start.1 = (bf16[256,1024]{1,0:T(8,128)(2,1)}, bf16[256,1024]{1,0:T(8,128)(2,1)S(1)}, u32[]{:S(2)}, u32[]{:S(2)}) collective-permute-start(bf16[256,1024]{1,0:T(8,128)(2,1)} %refs_0_), channel_id=1, source_target_pairs={{0,1},{1,0},{2,3},{3,2},{4,5},{5,4},{6,7},{7,6},{8,9},{9,8},{10,11... | collective-permute-start | bytes 1572872 | tf_op jit(solution)/shard_map/ppermute | solution.py:704
  3.4 22.5 %collective-permute-start = (bf16[256,1024]{1,0:T(8,128)(2,1)}, bf16[256,1024]{1,0:T(8,128)(2,1)S(1)}, u32[]{:S(2)}, u32[]{:S(2)}) collective-permute-start(bf16[256,1024]{1,0:T(8,128)(2,1)} %refs_0_), channel_id=1, source_target_pairs={{0,2},{1,3},{2,0},{3,1},{4,6},{5,7},{6,4},{7,5},{8,10},{9,11},{10,... | collective-permute-start | bytes 1572872 | tf_op jit(solution)/shard_map/ppermute | solution.py:703
  6.0 13.6 %all-to-all-start = ((bf16[8,80,128]{2,1,0:T(8,128)(2,1)}), bf16[8,80,128]{2,1,0:T(8,128)(2,1)S(1)}, u32[]{:S(2)}, u32[]{:S(2)}) async-start(bf16[8,80,128]{2,1,0:T(8,128)(2,1)} %get-tuple-element.36.query_far), calls=%async_computation | async-start | bytes 327680 | tf_op jit(solution)/shard_map/all_to_all | solution.py:705
  11.8 5.3 %copy-start.1 = (bf16[32,128,2,128]{3,2,1,0:T(2,128)(2,1)S(1)}, bf16[32,128,2,128]{3,2,1,0:T(2,128)(2,1)}, u32[]{:S(2)}) copy-start(bf16[32,128,2,128]{3,2,1,0:T(2,128)(2,1)} %param.21) | copy-start | bytes 6291460
  17.2 2.4 %copy-start.8 = (s32[8]{0:T(128)S(1)}, s32[8]{0:T(128)}, u32[]{:S(2)}) copy-start(s32[8]{0:T(128)} %lengths.1) | copy-start | bytes 100
  17.2 2.4 %copy-start.9 = (s32[256]{0:T(256)S(1)}, s32[256]{0:T(256)}, u32[]{:S(2)}) copy-start(s32[256]{0:T(256)} %homes.1) | copy-start | bytes 3076
  17.2 2.4 %copy-start.10 = (s32[256]{0:T(256)S(1)}, s32[256]{0:T(256)}, u32[]{:S(2)}) copy-start(s32[256]{0:T(256)} %pages.3) | copy-start | bytes 3076
  17.2 2.4 %copy-start.11 = (bf16[4,24,128]{2,1,0:T(8,128)(2,1)S(1)}, bf16[4,24,128]{2,1,0:T(8,128)(2,1)}, u32[]{:S(2)}) copy-start(bf16[4,24,128]{2,1,0:T(8,128)(2,1)} %tail.1) | copy-start | bytes 73732
  22.5 12.3 %all-to-all-start.1 = ((bf16[32,24,128]{2,1,0:T(8,128)(2,1)}), bf16[32,24,128]{2,1,0:T(8,128)(2,1)S(1)}, u32[]{:S(2)}, u32[]{:S(2)}) async-start(bf16[32,24,128]{2,1,0:T(8,128)(2,1)} %get-tuple-element.37), calls=%async_computation.1 | async-start | bytes 393216 | tf_op jit(solution)/shard_map/all_to_all | solution.py:737
  26.0 3.4 %collective-permute-start.2 = (bf16[256,1024]{1,0:T(8,128)(2,1)S(1)}, bf16[256,1024]{1,0:T(8,128)(2,1)S(1)}, u32[]{:S(2)}, u32[]{:S(2)}) collective-permute-start(bf16[256,1024]{1,0:T(8,128)(2,1)S(1)} %collective-permute-done.refs_2_), channel_id=1, source_target_pairs={{0,1},{1,0},{2,3},{3,2},{4,5},{5,4},{6,7},{7,6},{8,9},{9,8},{10,11... | collective-permute-start | bytes 1572872 | tf_op jit(solution)/shard_map/ppermute | solution.py:742
  29.8 5.7 %copy-start.3 = (bf16[256,1024]{1,0:T(8,128)(2,1)S(1)}, bf16[256,1024]{1,0:T(8,128)(2,1)}, u32[]{:S(2)}) copy-start(bf16[256,1024]{1,0:T(8,128)(2,1)} %refs_0_) | copy-start | bytes 1572868
  29.8 5.7 %copy-start.4 = (f32[3,1024]{1,0:T(4,128)S(1)}, f32[3,1024]{1,0:T(4,128)}, u32[]{:S(2)}) copy-start(f32[3,1024]{1,0:T(4,128)} %refs_4_.1) | copy-start | bytes 36868
  29.8 5.7 %copy-start.6 = (bf16[4,8,1024]{2,1,0:T(8,128)(2,1)S(1)}, bf16[4,8,1024]{2,1,0:T(8,128)(2,1)}, u32[]{:S(2)}) copy-start(bf16[4,8,1024]{2,1,0:T(8,128)(2,1)} %get-tuple-element.45.tokens) | copy-start | bytes 196612
  34.8 1.6 %copy-start.2 = (bf16[4,128,1024]{2,1,0:T(8,128)(2,1)S(1)}, bf16[4,128,1024]{2,1,0:T(8,128)(2,1)}, u32[]{:S(2)}) copy-start(bf16[4,128,1024]{2,1,0:T(8,128)(2,1)} %param.30) | copy-start | bytes 3145732
  34.8 15.3 %copy-start = (bf16[4,1024,256]{2,1,0:T(8,128)(2,1)S(1)}, bf16[4,1024,256]{2,1,0:T(8,128)(2,1)}, u32[]{:S(2)}) copy-start(bf16[4,1024,256]{2,1,0:T(8,128)(2,1)} %keep.1.first) | copy-start | bytes 6291460
  34.8 15.3 %copy-start.5 = (bf16[1024,32]{0,1:T(8,128)(2,1)S(1)}, bf16[1024,32]{0,1:T(8,128)(2,1)}, u32[]{:S(2)}) copy-start(bf16[1024,32]{0,1:T(8,128)(2,1)} %param.28) | copy-start | bytes 196612
  34.8 15.3 %collective-permute-start.3 = (bf16[4,1024,256]{2,1,0:T(8,128)(2,1)}, bf16[4,1024,256]{2,1,0:T(8,128)(2,1)S(1)}, u32[]{:S(2)}, u32[]{:S(2)}) collective-permute-start(bf16[4,1024,256]{2,1,0:T(8,128)(2,1)} %keep.1.first), channel_id=1, source_target_pairs={{0,1},{1,0},{2,3},{3,2},{4,5},{5,4},{6,7},{7,6},{8,9},{9,8},{10,11... | collective-permute-start | bytes 6291464 | tf_op jit(solution)/shard_map/ppermute | solution.py:777
  36.5 13.6 %collective-permute-start.4 = (bf16[512,1024]{1,0:T(8,128)(2,1)S(1)}, bf16[512,1024]{1,0:T(8,128)(2,1)S(1)}, u32[]{:S(2)}, u32[]{:S(2)}) collective-permute-start(bf16[512,1024]{1,0:T(8,128)(2,1)S(1)} %bitcast.28), channel_id=1, source_target_pairs={{0,1},{1,0},{2,3},{3,2},{4,5},{5,4},{6,7},{7,6},{8,9},{9,8},{10,11... | collective-permute-start | bytes 3145736 | tf_op jit(solution)/shard_map/ppermute | solution.py:792
  50.1 17.3 %copy-start.7 = (f32[1024]{0:T(1024)S(1)}, f32[1024]{0:T(1024)}, u32[]{:S(2)}) copy-start(f32[1024]{0:T(1024)} %param.31) | copy-start | bytes 12292
  63.4 3.4 %collective-permute-start.7 = (bf16[2,16,512]{2,1,0:T(8,128)(2,1)S(1)}, bf16[2,16,512]{2,1,0:T(8,128)(2,1)S(1)}, u32[]{:S(2)}, u32[]{:S(2)}) collective-permute-start(bf16[2,16,512]{2,1,0:T(8,128)(2,1)S(1)} %finish.1.refs_0_), channel_id=1, source_target_pairs={{0,3},{1,2},{2,1},{3,0},{4,7},{5,6},{6,5},{7,4},{8,11},{9,10},{10,... | collective-permute-start | bytes 98312 | tf_op jit(solution)/shard_map/ppermute | solution.py:824
  63.4 4.0 %collective-permute-start.6 = (bf16[2,16,512]{2,1,0:T(8,128)(2,1)S(1)}, bf16[2,16,512]{2,1,0:T(8,128)(2,1)S(1)}, u32[]{:S(2)}, u32[]{:S(2)}) collective-permute-start(bf16[2,16,512]{2,1,0:T(8,128)(2,1)S(1)} %finish.1.refs_0_), channel_id=1, source_target_pairs={{0,2},{1,3},{2,0},{3,1},{4,6},{5,7},{6,4},{7,5},{8,10},{9,11},{10,... | collective-permute-start | bytes 98312 | tf_op jit(solution)/shard_map/ppermute | solution.py:824
  64.1 3.4 %collective-permute-start.5 = (bf16[2,16,512]{2,1,0:T(8,128)(2,1)S(1)}, bf16[2,16,512]{2,1,0:T(8,128)(2,1)S(1)}, u32[]{:S(2)}, u32[]{:S(2)}) collective-permute-start(bf16[2,16,512]{2,1,0:T(8,128)(2,1)S(1)} %finish.1.refs_0_), channel_id=1, source_target_pairs={{0,1},{1,0},{2,3},{3,2},{4,5},{5,4},{6,7},{7,6},{8,9},{9,8},{10,11... | collective-permute-start | bytes 98312 | tf_op jit(solution)/shard_map/ppermute | solution.py:824
